TPU v7x, 32 devices: a whole 2x2x4 slice. The times are simulated.
32 devices in a mesh: ctx: 16 (over z, x, core), wsh: 2 (over y).
Axes of the slice: x: 2, y: 2, z: 4, core: 2. Of those that a mesh axis runs over, the one named last changes fastest.
Arguments:
- hidden_in: bfloat16 [2, 2, 8192, 768], P(None, 'wsh', 'ctx'), may hold values from -6 to 6
- segment_ids: int32 [2, 2, 8192], P(None, 'wsh'), may hold values from 0 to 10, never falling along the last dimension, each value on 1 to 1537 neighbouring positions
- out_grad: bfloat16 [2, 2, 8192, 768], P(None, 'wsh', 'ctx'), may hold values from -6 to 6
- query_w: bfloat16 [768, 384], P('wsh'), may hold values from -0.625 to 0.625
- query_b: bfloat16 [384], P('wsh'), may hold values from -3 to 3
- key_w: bfloat16 [768, 384], P('wsh'), may hold values from -0.21875 to 0.21875
- value_w: bfloat16 [768, 384], P('wsh'), may hold values from -0.21875 to 0.21875
- value_b: bfloat16 [384], P('wsh'), may hold values from -3 to 3
- depth_kernel: bfloat16 [9, 768], P(None, 'wsh'), may hold values from -2 to 2
- point_w: bfloat16 [768, 384], P('wsh'), may hold values from -0.21875 to 0.21875
- point_b: bfloat16 [384], P('wsh'), may hold values from -3 to 3
- kernel_w: bfloat16 [384, 54], P('wsh'), may hold values from -0.078125 to 0.078125
- kernel_b: bfloat16 [54], P('wsh'), may hold values from -3 to 3
- conv_w: bfloat16 [768, 384], P('wsh'), may hold values from -0.21875 to 0.21875
- conv_b: bfloat16 [384], P('wsh'), may hold values from -3 to 3
- output_w: bfloat16 [768, 768], P('wsh'), may hold values from -0.21875 to 0.21875
- output_b: bfloat16 [768], P('wsh'), may hold values from -3 to 3
- norm1_gain: bfloat16 [768], P('wsh'), may hold values from 0.5 to 1.5
- norm1_bias: bfloat16 [768], P('wsh'), may hold values from -3 to 3
- inner_w: bfloat16 [2, 384, 1536], P(None, 'wsh'), may hold values from -0.3125 to 0.3125
- inner_b: bfloat16 [3072], P('wsh'), may hold values from -3 to 3
- outer_w: bfloat16 [2, 1536, 384], P(None, 'wsh'), may hold values from -0.15625 to 0.15625
- outer_b: bfloat16 [768], P('wsh'), may hold values from -3 to 3
- norm2_gain: bfloat16 [768], P('wsh'), may hold values from 0.5 to 1.5
- norm2_bias: bfloat16 [768], P('wsh'), may hold values from -3 to 3
Outputs:
- output: bfloat16 [2, 2, 8192, 768], P(None, 'wsh', 'ctx')
- input_grad: float32 [2, 2, 8192, 768], P(None, 'wsh', 'ctx')
- grad_query_w: float32 [768, 384], P('wsh')
- grad_query_b: float32 [384], P('wsh')
- grad_key_w: float32 [768, 384], P('wsh')
- grad_value_w: float32 [768, 384], P('wsh')
- grad_value_b: float32 [384], P('wsh')
- grad_depth_kernel: float32 [9, 768], P(None, 'wsh')
- grad_point_w: float32 [768, 384], P('wsh')
- grad_point_b: float32 [384], P('wsh')
- grad_kernel_w: float32 [384, 54], P('wsh')
- grad_kernel_b: float32 [54], P('wsh')
- grad_conv_w: float32 [768, 384], P('wsh')
- grad_conv_b: float32 [384], P('wsh')
- grad_output_w: float32 [768, 768], P('wsh')
- grad_output_b: float32 [768], P('wsh')
- grad_norm1_gain: float32 [768], P('wsh')
- grad_norm1_bias: float32 [768], P('wsh')
- grad_inner_w: float32 [2, 384, 1536], P(None, 'wsh')
- grad_inner_b: float32 [3072], P('wsh')
- grad_outer_w: float32 [2, 1536, 384], P(None, 'wsh')
- grad_outer_b: float32 [768], P('wsh')
- grad_norm2_gain: float32 [768], P('wsh')
- grad_norm2_bias: float32 [768], P('wsh')
Inputs may be any that keep to these rules, and one draw needn't show every extreme that they name: `segment_ids`: within each sequence the document numbers never fall; each document has 1 to 1537 tokens, and one has exactly 1537.
All inputs are finite; a program needn't handle non-finite values.
Results may differ from a plain program's by a relative error of at most 0.015.
The roundings to bfloat16 on the way count: a program that leaves them out, or rounds other values in their place, can miss the bound.
Values may be sent and summed in bfloat16 or wider, within the bound.
A program may use at most 256 MiB of HBM per device.

v0:
```python
import functools
import types

import jax
import jax.numpy as jnp
from jax import lax
from jax.experimental import pallas as pl
from jax.experimental.pallas import tpu as pltpu
from jax.sharding import PartitionSpec as P

HEADS = 6
HEAD_DIM = 64
KERNEL = 9
GROUPS = 2


TILE = 256
NEG = -1000000000.0
LANES = 128
HEADS_HERE = HEADS // 2


def rows_nt(left, right):
    return lax.dot_general(
        left, right, (((1,), (1,)), ((), ())), preferred_element_type=jnp.float32
    )


def lane_half(block, upper):
    lane = lax.broadcasted_iota(jnp.int32, block.shape, 1)
    keep = lane >= HEAD_DIM if upper else lane < HEAD_DIM
    return jnp.where(keep, block, jnp.zeros_like(block))


def same_document(segk_ref, segq_ref, rows):
    row = segk_ref[0:1, rows]
    column = jnp.broadcast_to(row, (LANES, row.shape[1])).T
    wide = jnp.concatenate([column] * (TILE // LANES), axis=1)
    return wide == segq_ref[0:1, :]


def load_queries(q_ref, qm_ref):
    scale = jnp.asarray(HEAD_DIM ** (-0.5), q_ref.dtype)
    first = q_ref[:, 0:LANES] * scale
    qm_ref[0] = lane_half(first, False)
    qm_ref[1] = lane_half(first, True)
    qm_ref[2] = lane_half(q_ref[:, LANES : 2 * LANES] * scale, False)


KEY_GROUP = (0, 0, 1)
VALUE_GROUP = (2, 2, 1)


def lane_group(group):
    return slice(group * LANES, (group + 1) * LANES)


def over_tiles(first, last, step):
    fours = lax.div(last - first, 4)

    def four(p, carry):
        step(first + 4 * p, 4)
        return carry

    lax.fori_loop(0, fours, four, 0)
    rest = last - first - 4 * fours
    at = first + 4 * fours

    @pl.when(rest >= 2)
    def _():
        step(at, 2)

    @pl.when(lax.rem(rest, 2) == 1)
    def _():
        step(last - 1, 1)


def attend_kernel(bounds, q_ref, kv_ref, segk_ref, segq_ref, out_ref, outt_ref, lse_ref,
                  qm_ref, m_ref, l_ref, acc_ref):
    tile = pl.program_id(0)
    load_queries(q_ref, qm_ref)
    m_ref[...] = jnp.full_like(m_ref, -jnp.inf)
    l_ref[...] = jnp.zeros_like(l_ref)
    acc_ref[...] = jnp.zeros_like(acc_ref)

    def step(j, tiles):
        rows = pl.ds(pl.multiple_of(j * TILE, TILE), tiles * TILE)
        same = same_document(segk_ref, segq_ref, rows)
        values_t = kv_ref[rows, LANES : 3 * LANES].T
        value_rows = (2 * HEAD_DIM, 3 * HEAD_DIM, HEAD_DIM)
        raw = [
            rows_nt(kv_ref[rows, lane_group(KEY_GROUP[head])], qm_ref[head])
            for head in range(HEADS_HERE)
        ]
        highs, alphas = [], []
        for head in range(HEADS_HERE):
            scores = jnp.where(same, raw[head], NEG)
            old = m_ref[head : head + 1, :]
            top = jnp.maximum(old, jnp.max(scores, axis=0, keepdims=True))
            expo = jnp.exp(scores - top)
            alpha = jnp.exp(old - top)
            m_ref[head : head + 1, :] = top
            l_ref[head : head + 1, :] = l_ref[head : head + 1, :] * alpha + jnp.sum(
                expo, axis=0, keepdims=True
            )
            high = expo.astype(jnp.bfloat16)
            highs.append(high)
            alphas.append(alpha)
        for head in range(HEADS_HERE):
            span = slice(head * HEAD_DIM, (head + 1) * HEAD_DIM)
            vals = values_t[value_rows[head] : value_rows[head] + HEAD_DIM, :]
            acc_ref[span, :] = acc_ref[span, :] * alphas[head] + jnp.dot(
                vals, highs[head], preferred_element_type=jnp.float32
            )

    over_tiles(bounds[0, tile], bounds[1, tile], step)
    lse_ref[...] = m_ref[...] + jnp.log(l_ref[...])
    used = HEADS_HERE * HEAD_DIM
    for head in range(HEADS_HERE):
        span = slice(head * HEAD_DIM, (head + 1) * HEAD_DIM)
        inv = 1.0 / l_ref[head : head + 1, :]
        acc_ref[span, :] = acc_ref[span, :] * inv
    outt_ref[...] = acc_ref[...]
    out_ref[...] = acc_ref[...].T.astype(jnp.bfloat16)


def attend(bounds, queries, window, seg_keys, seg_queries):
    rows, wide = queries.shape
    span, width = window.shape
    return pl.pallas_call(
        attend_kernel,
        grid_spec=pltpu.PrefetchScalarGridSpec(
            num_scalar_prefetch=1,
            grid=(rows // TILE,),
            in_specs=[
                pl.BlockSpec((TILE, wide), lambda i, b: (i, 0)),
                pl.BlockSpec((span, width), lambda i, b: (0, 0)),
                pl.BlockSpec((1, span), lambda i, b: (0, 0)),
                pl.BlockSpec((1, TILE), lambda i, b: (0, i)),
            ],
            out_specs=[
                pl.BlockSpec((TILE, wide), lambda i, b: (i, 0)),
                pl.BlockSpec((wide, TILE), lambda i, b: (0, i)),
                pl.BlockSpec((8, TILE), lambda i, b: (0, i)),
            ],
            scratch_shapes=[
                pltpu.VMEM((HEADS_HERE, TILE, LANES), jnp.bfloat16),
                pltpu.VMEM((8, TILE), jnp.float32),
                pltpu.VMEM((8, TILE), jnp.float32),
                pltpu.VMEM((wide, TILE), jnp.float32),
            ],
        ),
        out_shape=[
            jax.ShapeDtypeStruct((rows, wide), jnp.bfloat16),
            jax.ShapeDtypeStruct((wide, rows), jnp.float32),
            jax.ShapeDtypeStruct((8, rows), jnp.float32),
        ],
        compiler_params=pltpu.CompilerParams(vmem_limit_bytes=63 * 2**20),
        name="attend",
    )(bounds, queries, window, seg_keys, seg_queries)


def attend_back_kernel(bounds, q_ref, kv_ref, segk_ref, segq_ref, grad_ref, outt_ref, lse_ref,
                       dq_ref, dkv_ref, qm_ref, gm_ref, delta_ref, dq_acc, dkv_acc):
    tile = pl.program_id(0)

    @pl.when(tile == 0)
    def _():
        dkv_acc[...] = jnp.zeros_like(dkv_acc)

    load_queries(q_ref, qm_ref)
    gm_ref[0] = lane_half(grad_ref[:, 0:LANES], False)
    gm_ref[1] = lane_half(grad_ref[:, 0:LANES], True)
    gm_ref[2] = lane_half(grad_ref[:, LANES : 2 * LANES], True)
    grads_t = grad_ref[...].astype(jnp.float32).T
    grad_rows = (0, HEAD_DIM, 3 * HEAD_DIM)
    for head in range(HEADS_HERE):
        span = slice(head * HEAD_DIM, (head + 1) * HEAD_DIM)
        delta_ref[head : head + 1, :] = jnp.sum(
            grads_t[grad_rows[head] : grad_rows[head] + HEAD_DIM, :] * outt_ref[span, :],
            axis=0, keepdims=True,
        )
    dq_acc[...] = jnp.zeros_like(dq_acc)

    def step(j, tiles):
        rows = pl.ds(pl.multiple_of(j * TILE, TILE), tiles * TILE)
        same = same_document(segk_ref, segq_ref, rows)
        keys_t = kv_ref[rows, 0 : 2 * LANES].T
        sums = [dkv_acc[rows, lane_group(g)] for g in range(3)]
        raw = [
            rows_nt(kv_ref[rows, lane_group(KEY_GROUP[head])], qm_ref[head])
            for head in range(HEADS_HERE)
        ]
        draw = [
            rows_nt(kv_ref[rows, lane_group(VALUE_GROUP[head])], gm_ref[head])
            for head in range(HEADS_HERE)
        ]
        ps, dss = [], []
        for head in range(HEADS_HERE):
            probs = jnp.where(same, jnp.exp(raw[head] - lse_ref[head : head + 1, :]), 0.0)
            dss.append((probs * (draw[head] - delta_ref[head : head + 1, :])).astype(jnp.bfloat16))
            ps.append(probs.astype(jnp.bfloat16))
        for head in range(HEADS_HERE):
            span = slice(head * HEAD_DIM, (head + 1) * HEAD_DIM)
            dq_acc[span, :] += jnp.dot(
                keys_t[span, :], dss[head], preferred_element_type=jnp.float32
            )
            sums[KEY_GROUP[head]] += jnp.dot(
                dss[head], qm_ref[head], preferred_element_type=jnp.float32
            )
            sums[VALUE_GROUP[head]] += jnp.dot(
                ps[head], gm_ref[head], preferred_element_type=jnp.float32
            )
        for g in range(3):
            dkv_acc[rows, lane_group(g)] = sums[g]

    over_tiles(bounds[0, tile], bounds[1, tile], step)
    dq_ref[...] = (dq_acc[...].T * HEAD_DIM ** (-0.5)).astype(dq_ref.dtype)

    @pl.when(tile == pl.num_programs(0) - 1)
    def _():
        dkv_ref[...] = dkv_acc[...].astype(dkv_ref.dtype)


def attend_back(bounds, queries, window, seg_keys, seg_queries, grads, outt, lse):
    rows, wide = queries.shape
    span, width = window.shape
    return pl.pallas_call(
        attend_back_kernel,
        grid_spec=pltpu.PrefetchScalarGridSpec(
            num_scalar_prefetch=1,
            grid=(rows // TILE,),
            in_specs=[
                pl.BlockSpec((TILE, wide), lambda i, b: (i, 0)),
                pl.BlockSpec((span, width), lambda i, b: (0, 0)),
                pl.BlockSpec((1, span), lambda i, b: (0, 0)),
                pl.BlockSpec((1, TILE), lambda i, b: (0, i)),
                pl.BlockSpec((TILE, wide), lambda i, b: (i, 0)),
                pl.BlockSpec((wide, TILE), lambda i, b: (0, i)),
                pl.BlockSpec((8, TILE), lambda i, b: (0, i)),
            ],
            out_specs=[
                pl.BlockSpec((TILE, wide), lambda i, b: (i, 0)),
                pl.BlockSpec((span, width), lambda i, b: (0, 0)),
            ],
            scratch_shapes=[
                pltpu.VMEM((HEADS_HERE, TILE, LANES), jnp.bfloat16),
                pltpu.VMEM((HEADS_HERE, TILE, LANES), jnp.bfloat16),
                pltpu.VMEM((8, TILE), jnp.float32),
                pltpu.VMEM((wide, TILE), jnp.float32),
                pltpu.VMEM((span, width), jnp.float32),
            ],
        ),
        out_shape=[
            jax.ShapeDtypeStruct((rows, wide), jnp.bfloat16),
            jax.ShapeDtypeStruct((span, width), jnp.bfloat16),
        ],
        compiler_params=pltpu.CompilerParams(vmem_limit_bytes=63 * 2**20),
        name="attend_back",
    )(bounds, queries, window, seg_keys, seg_queries, grads, outt, lse)


def rolled(part):
    return jnp.concatenate([part[..., HEAD_DIM:], part[..., :HEAD_DIM]], axis=-1)


def joined_halves(lower, upper):
    return jnp.concatenate([lower[..., :HEAD_DIM], upper[..., HEAD_DIM:]], axis=-1)


def lanes_of(values):
    return [values[..., lane_group(g)] for g in range(3)]


def parts_of_queries(queries, upper):
    one, two, three = lanes_of(queries)
    swapped = rolled(two)
    first, second = (swapped, two) if upper else (two, swapped)
    return jnp.stack(
        [jnp.concatenate([one, first], axis=-1), jnp.concatenate([three, second], axis=-1)], axis=1
    ).reshape(TEAM, queries.shape[1], 2 * LANES)


def parts_of_keys(keys, values):
    k = lanes_of(keys)
    v = lanes_of(values)
    low = jnp.concatenate([k[0], joined_halves(k[1], rolled(v[1])), v[0]], axis=-1)
    high = jnp.concatenate([k[2], joined_halves(rolled(k[1]), v[1]), v[2]], axis=-1)
    return jnp.stack([low, high], axis=1).reshape(TEAM, keys.shape[1], 3 * LANES)


def natural_rows(parts):
    pairs = parts.reshape(TEAM // 2, 2, parts.shape[1], 2 * LANES)
    low, high = pairs[:, 0], pairs[:, 1]
    middle = joined_halves(low[..., LANES:], rolled(high[..., LANES:]))
    return jnp.concatenate([low[..., :LANES], middle, high[..., :LANES]], axis=-1)


def natural_keys(parts):
    pairs = parts.reshape(TEAM // 2, 2, parts.shape[1], 3 * LANES)
    low, high = lanes_of(pairs[:, 0]), lanes_of(pairs[:, 1])
    keys = jnp.concatenate([low[0], joined_halves(low[1], rolled(high[1])), high[0]], axis=-1)
    values = jnp.concatenate([low[2], joined_halves(rolled(low[1]), high[1]), high[2]], axis=-1)
    return keys, values


TEAM = 4


def flip(index, step):
    return index + step * (1 - 2 * lax.rem(lax.div(index, step), 2))


def mate(rank, offset):
    if offset % 2:
        rank = flip(rank, 1)
    if offset // 2:
        rank = flip(rank, 2)
    return rank


def greet(peers):
    barrier = pltpu.get_barrier_semaphore()
    for peer in peers:
        pl.semaphore_signal(
            barrier, inc=1, device_id=peer, device_id_type=pl.DeviceIdType.MESH
        )
    pl.semaphore_wait(barrier, len(peers))


def remote(src, dst, send, recv, peer):
    return pltpu.make_async_remote_copy(
        src_ref=src,
        dst_ref=dst,
        send_sem=send,
        recv_sem=recv,
        device_id=peer,
        device_id_type=pl.DeviceIdType.MESH,
    )


RIM = 16
SMALL_ROWS = 128
SMALL_IN = 128
ROW_IN_KERNEL_W = 32
ROW_PAIR_QV, ROW_PAIR_PC, ROW_IN_KERNEL_B = 19, 20, 21
ROW_OUTPUT_B, ROW_GAIN1, ROW_SHIFT1, ROW_OUTER_B, ROW_GAIN2, ROW_SHIFT2 = range(9, 15)
ROW_INNER_B = 15
ROW_QUERY_B, ROW_VALUE_B, ROW_POINT_B, ROW_CONV_B = range(19, 23)
ROW_KERNEL_B = 24
ROW_KERNEL_W = 48
TAP_ROWS = 8 * KERNEL


def dot(left, right):
    return jnp.dot(left, right, preferred_element_type=jnp.float32)


def dot_tn(left, right):
    return lax.dot_general(
        left, right, (((0,), (0,)), ((), ())), preferred_element_type=jnp.float32
    )


def half_turn(block):
    return pltpu.roll(block, HEAD_DIM, axis=1)


def mixed_lanes(lower, upper):
    lane = lax.broadcasted_iota(jnp.int32, lower.shape, 1)
    return jnp.where(lane < HEAD_DIM, lower, upper)


def pair_row(small_ref, row, second):
    first = jnp.broadcast_to(small_ref[0, row : row + 1, :], (8, 384))
    other = jnp.broadcast_to(small_ref[1, row : row + 1, :], (8, 384))
    lane = lax.broadcasted_iota(jnp.int32, first.shape, 1)
    if second:
        first = pltpu.roll(first, 192, axis=1)
    else:
        other = pltpu.roll(other, 192, axis=1)
    return jnp.where(lane < 192, first, other)[0:1, :]


def tap_major(shape, offset):
    row = lax.broadcasted_iota(jnp.int32, shape, 0)
    column = lax.broadcasted_iota(jnp.int32, shape, 1) + offset
    head = lax.rem(row, 8)
    wanted = (head * KERNEL + lax.div(row, 8) == column) & (head < HEADS)
    return wanted & (row < TAP_ROWS)


def kernel_rows(first, other):
    lane = lax.broadcasted_iota(jnp.int32, first.shape, 1)
    rows = jnp.where(lane < 192, first, pltpu.roll(other, 192, axis=1))
    return jnp.concatenate(
        [rows, jnp.zeros((LANES - TAP_ROWS, rows.shape[1]), jnp.float32)], axis=0
    ).astype(jnp.bfloat16)


def kernel_bias(small_ref):
    half = HEADS * KERNEL // 2
    total = jnp.zeros((LANES, 1), jnp.float32)
    for w in range(2):
        row = small_ref[w, ROW_IN_KERNEL_B : ROW_IN_KERNEL_B + 1, 0:LANES]
        lane = lax.broadcasted_iota(jnp.int32, (LANES, LANES), 1)
        wanted = tap_major((LANES, LANES), w * half) & (lane < half)
        total = total + jnp.sum(jnp.where(wanted, row, 0.0), axis=1, keepdims=True)
    return total


def rows_of(ref, base, count):
    view = pl.ds(pl.multiple_of(base, 16), count)
    return ref.at[:, view, :] if len(ref.shape) == 3 else ref.at[view, :]


CHUNKS = 4


def front_kernel(count, *refs):
    x_ref, seg_ref, mask_ref, depth_in, kernel_in, kernel_b_in = refs[:6]
    vectors, pairs = refs[6:13], refs[13:17]
    shards = list(refs[17 : 16 + count])
    outer_any = refs[16 + count]
    rest = refs[17 + count :]
    outs = rest[: count + 9]
    half_any = rest[count + 9]
    win_ref, qteam_ref = outs[count : count + 2]
    holds = rest[count + 10 : 2 * count + 17]
    fulls = holds[:count]
    queries_ref, xrim_ref, depth_ref, spans_ref, kern_ref, ext_ref, conv_ref = holds[count:]
    (kv_part, q_part, seg_col, halo_low, halo_high, spread_ref, taps_ref, wide_ref,
     send_y, recv_y, send_c, recv_c, local, send_h, recv_h, send_kv, recv_kv, send_q, recv_q,
     send_l, recv_l, send_r, recv_r, emit_sem, small_f32, small_own, outer_half, half_sem) = rest[
        2 * count + 17 :
    ]
    shards.insert(2, small_own)
    key_ref, value_ref, small2d, query_ref, point_ref, convw_ref = fulls[:6]
    me, side = lax.axis_index("ctx"), lax.axis_index("wsh")
    size = lax.axis_size("ctx")
    core = lax.rem(me, 2)
    rank = lax.rem(me, TEAM)
    chip = lax.div(rank, 2)
    base = me - rank
    team = lax.div(me, TEAM)
    teams = size // TEAM
    right, left = lax.rem(me + TEAM, size), lax.rem(me + size - TEAM, size)
    after, prior = lax.rem(me + 1, size), lax.rem(me + size - 1, size)
    twin, across = {"ctx": flip(me, 1)}, {"wsh": 1 - side}
    seqs, block, model = x_ref.shape
    halo = (TEAM - 1) * block
    width = HEADS * HEAD_DIM
    chunk_rows = block // CHUNKS
    greet(
        [{"ctx": base + mate(rank, o)} for o in range(1, TEAM)]
        + [across, {"ctx": right}, {"ctx": left}, {"ctx": after}, {"ctx": prior}]
    )

    to_y, passed, own, emitted = [], [], [], []
    for i in range(count):
        rows = shards[i].shape[-2]
        to_y.append(
            remote(
                rows_of(shards[i], core * (rows // 2), rows // 2),
                rows_of(fulls[i], side * rows + core * (rows // 2), rows // 2),
                send_y.at[i], recv_y.at[i], across,
            )
        )
        came = rows_of(fulls[i], (1 - side) * rows + core * (rows // 2), rows // 2)
        passed.append(remote(came, came, send_c.at[i], recv_c.at[i], twin))
        own.append(
            pltpu.make_async_copy(shards[i], rows_of(fulls[i], side * rows, rows), local.at[i])
        )

    def emit(hold, out):
        copy = pltpu.make_async_copy(hold, out, emit_sem.at[len(emitted)])
        copy.start()
        emitted.append(copy)

    def emit_named(k):
        emit(holds[count + k], outs[count + 2 + k])

    urgent = 3
    for i in range(2):
        to_y[i].start()
    for i in range(2):
        own[i].start()
    half_rows = outer_half.shape[1]
    load_half = pltpu.make_async_copy(
        outer_any.at[:, part_rows(core * half_rows, half_rows), :], outer_half, half_sem.at[0]
    )
    load_half.start()
    small_f32[...] = jnp.zeros_like(small_f32)
    small_f32[0:KERNEL, :] = depth_in[...].astype(jnp.float32)

    def as_row(ref):
        return ref[...].astype(jnp.float32).reshape(1, ref.shape[0])

    at = KERNEL
    for ref in vectors:
        row = as_row(ref)
        for k in range(ref.shape[0] // 384):
            small_f32[at : at + 1, :] = row[:, k * 384 : (k + 1) * 384]
            at += 1
    for k in range(2):
        small_f32[at : at + 1, 0:192] = as_row(pairs[2 * k])
        small_f32[at : at + 1, 192:384] = as_row(pairs[2 * k + 1])
        at += 1
    small_f32[at : at + 1, 0 : kernel_b_in.shape[0]] = as_row(kernel_b_in)
    pick = jnp.where(tap_major((LANES, HEADS * KERNEL), 0), 1.0, 0.0).astype(jnp.bfloat16)
    small_f32[ROW_IN_KERNEL_W : ROW_IN_KERNEL_W + TAP_ROWS, 0:192] = dot(pick, kernel_in[...])[
        0:TAP_ROWS, :
    ]
    small_own[...] = small_f32[...].astype(jnp.bfloat16)
    to_y[2].start()
    own[2].start()
    to_after = remote(x_ref.at[:, pl.ds(block - RIM, RIM), :], halo_low, send_h.at[0],
                      recv_h.at[0], {"ctx": after})
    to_prior = remote(x_ref.at[:, pl.ds(0, RIM), :], halo_high, send_h.at[1], recv_h.at[1],
                      {"ctx": prior})
    pl.when(me < size - 1)(to_after.start)
    pl.when(me > 0)(to_prior.start)
    to_y[urgent].start()
    own[urgent].start()

    @pl.when(me == 0)
    def _():
        halo_low[...] = jnp.zeros_like(halo_low)

    @pl.when(me == size - 1)
    def _():
        halo_high[...] = jnp.zeros_like(halo_high)

    for s in range(seqs):
        seg_col[s] = jnp.broadcast_to(seg_ref[s : s + 1, :], (LANES, seg_ref.shape[1])).T
        for g in range(model // LANES):
            xrim_ref[s, g, pl.ds(RIM, block), :] = x_ref[s, :, lane_group(g)].astype(jnp.float32)

    def arrive(i):
        to_y[i].wait_recv()
        passed[i].start()

    def settle(i):
        own[i].wait()
        passed[i].wait_recv()
        emit(fulls[i], outs[i])

    for i in range(urgent):
        arrive(i)
    for i in (4, 5, 6, 7):
        to_y[i].start()
        own[i].start()
    for i in range(urgent):
        settle(i)
    small_ref = taps_ref
    for w in range(2):
        small_ref[w] = small2d[pl.ds(w * SMALL_IN, SMALL_IN), :].astype(jnp.float32)
    value_bias = pair_row(small_ref, ROW_PAIR_QV, True)
    query_bias = pair_row(small_ref, ROW_PAIR_QV, False)

    def piece(r, c):
        return win_ref.at[
            pl.ds(pl.multiple_of(halo + r * block + c * chunk_rows, 16), chunk_rows), :
        ]

    def part(r, c):
        return kv_part.at[r, pl.ds(c * chunk_rows, chunk_rows), :]

    def kv_copy(r, c):
        return (
            pltpu.make_async_copy(part(r, c), piece(rank, c), recv_kv.at[rank * CHUNKS + c]),
            remote(part(r, c), piece(rank, c), send_kv.at[r * CHUNKS + c],
                   recv_kv.at[rank * CHUNKS + c], {"ctx": base + r}),
        )

    def q_copy(r):
        return (
            pltpu.make_async_copy(q_part.at[r], qteam_ref.at[rank], recv_q.at[rank]),
            remote(q_part.at[r], qteam_ref.at[rank], send_q.at[r], recv_q.at[rank],
                   {"ctx": base + r}),
        )

    def begin(pair, r):
        pl.when(rank == r)(pair[0].start)
        pl.when(rank != r)(pair[1].start)

    for s in (1 - chip, chip):
        rows = x_ref[s]
        keys = dot(rows, key_ref[...])
        values = dot(rows, value_ref[...]) + value_bias
        k = [keys[:, lane_group(g)] for g in range(3)]
        v = [values[:, lane_group(g)] for g in range(3)]
        for half, groups in enumerate((
            (k[0], mixed_lanes(k[1], half_turn(v[1])), v[0]),
            (k[2], mixed_lanes(half_turn(k[1]), v[1]), v[2]),
        )):
            for g in range(3):
                kv_part[2 * s + half, :, lane_group(g)] = groups[g].astype(jnp.bfloat16)
        for c in range(CHUNKS):
            for half in range(2):
                begin(kv_copy(2 * s + half, c), 2 * s + half)

    def onward(r, c):
        to_right = remote(
            piece(r, c),
            win_ref.at[
                pl.ds(pl.multiple_of(lax.rem(r + TEAM - 1, TEAM) * block + c * chunk_rows, 16),
                      chunk_rows), :
            ],
            send_r.at[r * CHUNKS + c], recv_r.at[r * CHUNKS + c], {"ctx": right},
        )
        to_left = remote(
            piece(r, c),
            win_ref.at[
                pl.ds(
                    pl.multiple_of(
                        halo + TEAM * block + lax.rem(r, TEAM - 1) * block + c * chunk_rows, 16
                    ),
                    chunk_rows,
                ), :
            ],
            send_l.at[r * CHUNKS + c], recv_l.at[r * CHUNKS + c], {"ctx": left},
        )
        return to_right, to_left

    def relay(o, c):
        r = mate(rank, o)
        if o == 0:
            kv_copy(r, c)[0].wait()
        else:
            remote(part(rank, c), piece(r, c), send_kv.at[rank * CHUNKS + c],
                   recv_kv.at[r * CHUNKS + c], {"ctx": base + r}).wait_recv()
        to_right, to_left = onward(r, c)
        pl.when((r >= 1) & (team < teams - 1))(to_right.start)
        pl.when((r <= TEAM - 2) & (team > 0))(to_left.start)

    for c in range(CHUNKS):
        relay(0, c)
        relay(1, c)
    arrive(urgent)
    settle(urgent)
    for s in range(seqs):
        queries = dot(x_ref[s], query_ref[...]) + query_bias
        queries_ref[s] = queries.astype(jnp.bfloat16)
        q = [queries[:, lane_group(g)] for g in range(3)]
        for half, groups in enumerate(((q[0], q[1]), (q[2], half_turn(q[1])))):
            for g in range(2):
                q_part[2 * s + half, :, lane_group(g)] = groups[g].astype(jnp.bfloat16)
        for half in range(2):
            begin(q_copy(2 * s + half), 2 * s + half)
    emit_named(0)

    pl.when(me > 0)(to_after.wait_recv)
    pl.when(me < size - 1)(to_prior.wait_recv)
    for s in range(seqs):
        for g in range(model // LANES):
            xrim_ref[s, g, pl.ds(0, RIM), :] = halo_low[s, :, lane_group(g)].astype(jnp.float32)
            xrim_ref[s, g, pl.ds(RIM + block, RIM), :] = halo_high[s, :, lane_group(g)].astype(
                jnp.float32
            )
    emit_named(1)
    strip = 32
    lead = RIM - KERNEL // 2

    def taps_row(j, g):
        return small_ref[g // 3, j : j + 1, lane_group(g % 3)]

    def depth_strip(c, s):
        start = c * strip
        here = seg_col[s, pl.ds(RIM + start, strip), :]
        sums = [jnp.zeros((strip, LANES), jnp.float32) for _ in range(model // LANES)]
        for j in range(KERNEL):
            same = seg_col[s, pl.ds(lead + j + start, strip), :] == here
            for g in range(model // LANES):
                near = xrim_ref[s, g, pl.ds(lead + j + start, strip), :]
                sums[g] = sums[g] + jnp.where(same, near, 0.0) * taps_row(j, g)
        for g in range(model // LANES):
            depth_ref[s, pl.ds(pl.multiple_of(start, strip), strip), lane_group(g)] = sums[
                g
            ].astype(jnp.bfloat16)
        return s

    relay(2, 0)
    relay(3, 0)
    lax.fori_loop(0, block // strip, depth_strip, 0)
    relay(2, 1)
    relay(3, 1)
    lax.fori_loop(0, block // strip, depth_strip, 1)
    emit_named(2)
    for c in range(2, CHUNKS):
        relay(2, c)
        relay(3, c)
    for j in range(KERNEL):
        row = lax.broadcasted_iota(jnp.int32, (2 * LANES, width), 0)
        col = lax.broadcasted_iota(jnp.int32, (2 * LANES, width), 1)
        row = jnp.where(row >= LANES, row - LANES, row)
        spread_ref[j] = jnp.where(row == 8 * j + col // HEAD_DIM, 1.0, 0.0).astype(jnp.bfloat16)
    for i in (4, 5):
        arrive(i)
    for i in (4, 5):
        settle(i)
    load_half.wait()
    emit(outer_half, half_any)
    point_bias = pair_row(small_ref, ROW_PAIR_PC, False)
    conv_bias = pair_row(small_ref, ROW_PAIR_PC, True)
    tap_view = slice(ROW_IN_KERNEL_W, ROW_IN_KERNEL_W + TAP_ROWS)
    kernel_w = kernel_rows(small_ref[0, tap_view, :], small_ref[1, tap_view, :])
    kernel_b = kernel_bias(small_ref)
    for s in range(seqs):
        spans = dot(depth_ref[s], point_ref[...]) + point_bias
        spans_ref[s] = spans
        mixed = (spans * queries_ref[s].astype(jnp.float32)).astype(jnp.bfloat16)
        logits = rows_nt(kernel_w, mixed) + kernel_b
        cut = [logits[8 * j : 8 * j + 8, :] for j in range(KERNEL)]
        top = functools.reduce(jnp.maximum, cut)
        expo = [jnp.exp(part - top) for part in cut]
        inverse = 1.0 / sum(expo)
        for j in range(KERNEL):
            kern = expo[j] * inverse
            kern_ref[s, 8 * j : 8 * j + 8, :] = kern
            wide_ref[8 * j : 8 * j + 8, :] = kern * mask_ref[s, j : j + 1, :]
        wide_ref[TAP_ROWS:, :] = jnp.zeros((LANES - TAP_ROWS, block), jnp.float32)
        tall = wide_ref[...].T
        high = tall.astype(jnp.bfloat16)
        low = (tall - high.astype(jnp.float32)).astype(jnp.bfloat16)
        both = jnp.concatenate([high, low], axis=1)
        for g in range(3):
            row_ext = [xrim_ref[s, k] for k in range(model // LANES)]
        ext = dot(
            jnp.concatenate([part.astype(jnp.bfloat16) for part in row_ext], axis=1),
            convw_ref[...],
        ) + conv_bias
        for g in range(3):
            ext_ref[s, g] = ext[:, lane_group(g)]
        chunk = 128
        for c in range(block // chunk):
            sums = [jnp.zeros((chunk, LANES), jnp.float32) for _ in range(3)]
            for j in range(KERNEL):
                weight = dot(both[c * chunk : (c + 1) * chunk, :], spread_ref[j])
                for g in range(3):
                    near = ext_ref[s, g, pl.ds(lead + j + c * chunk, chunk), :]
                    sums[g] = sums[g] + weight[:, lane_group(g)] * near
            for g in range(3):
                conv_ref[s, pl.ds(c * chunk, chunk), lane_group(g)] = sums[g].astype(jnp.bfloat16)

    for k in range(3, 7):
        emit_named(k)
    for i in (6, 7):
        arrive(i)
    for i in (6, 7):
        settle(i)
    for r in range(TEAM):
        for c in range(CHUNKS):
            pl.when(rank != r)(kv_copy(r, c)[1].wait_send)
        pl.when(rank != r)(q_copy(r)[1].wait_send)
    for o in range(TEAM):
        r = mate(rank, o)
        if o == 0:
            q_copy(r)[0].wait()
        else:
            remote(q_part.at[rank], qteam_ref.at[r], send_q.at[rank], recv_q.at[r],
                   {"ctx": base + r}).wait_recv()
    for r in range(TEAM):
        for c in range(CHUNKS):
            to_right, to_left = onward(jnp.int32(r), c)
            if r >= 1:
                pl.when(team < teams - 1)(to_right.wait_send)
                pl.when(team > 0)(to_right.wait_recv)
            if r <= TEAM - 2:
                pl.when(team > 0)(to_left.wait_send)
                pl.when(team < teams - 1)(to_left.wait_recv)
    for i in range(count):
        to_y[i].wait_send()
        passed[i].wait_send()
    pl.when(me < size - 1)(to_after.wait_send)
    pl.when(me > 0)(to_prior.wait_send)
    for copy in emitted:
        copy.wait()


def front(hidden, seg_rim, tap_mask, depth, kernel, kernel_b, vectors, pairs, shards, outer):
    seqs, block, model = hidden.shape
    small = jax.ShapeDtypeStruct((SMALL_IN, 384), hidden.dtype)
    gathered = list(shards[:2]) + [small] + list(shards[2:])
    count = len(gathered)
    half = jax.ShapeDtypeStruct((outer.shape[0], outer.shape[1] // 2, outer.shape[2]), outer.dtype)
    width = HEADS * HEAD_DIM
    wide = block + 2 * RIM
    fulls = [
        jax.ShapeDtypeStruct(s.shape[:-2] + (2 * s.shape[-2], s.shape[-1]), s.dtype) for s in gathered
    ]
    vmem = pl.BlockSpec(memory_space=pltpu.VMEM)
    anywhere = pl.BlockSpec(memory_space=pl.ANY)
    low, full = jnp.bfloat16, jnp.float32
    outs = [
        jax.ShapeDtypeStruct(((3 * TEAM - 2) * block, width), low),
        jax.ShapeDtypeStruct((TEAM, block, 2 * LANES), low),
        jax.ShapeDtypeStruct((seqs, block, width), low),
        jax.ShapeDtypeStruct((seqs, model // LANES, wide, LANES), full),
        jax.ShapeDtypeStruct((seqs, block, model), low),
        jax.ShapeDtypeStruct((seqs, block, width), full),
        jax.ShapeDtypeStruct((seqs, TAP_ROWS, block), full),
        jax.ShapeDtypeStruct((seqs, 3, wide, LANES), full),
        jax.ShapeDtypeStruct((seqs, block, width), low),
    ]
    dma = pltpu.SemaphoreType.DMA
    return pl.pallas_call(
        functools.partial(front_kernel, count),
        out_shape=fulls + outs + [half],
        in_specs=[vmem] * 17 + [anywhere] * count,
        out_specs=[anywhere] * (count + 10),
        scratch_shapes=[pltpu.VMEM(s.shape, s.dtype) for s in fulls + outs[2:]] + [
            pltpu.VMEM((TEAM, block, width), low),
            pltpu.VMEM((TEAM, block, 2 * LANES), low),
            pltpu.VMEM((seqs, seg_rim.shape[1], LANES), full),
            pltpu.VMEM((seqs, RIM, model), low),
            pltpu.VMEM((seqs, RIM, model), low),
            pltpu.VMEM((KERNEL, 2 * LANES, width), low),
            pltpu.VMEM((2, SMALL_IN, 384), full),
            pltpu.VMEM((LANES, block), full),
            dma((count,)), dma((count,)), dma((count,)), dma((count,)), dma((count,)),
            dma((2,)), dma((2,)),
            dma((TEAM * CHUNKS,)), dma((TEAM * CHUNKS,)), dma((TEAM,)), dma((TEAM,)),
            dma((TEAM * CHUNKS,)), dma((TEAM * CHUNKS,)), dma((TEAM * CHUNKS,)),
            dma((TEAM * CHUNKS,)), dma((count + 8,)),
            pltpu.VMEM((SMALL_IN, 384), full), pltpu.VMEM((SMALL_IN, 384), low),
            pltpu.VMEM(half.shape, low), dma((1,)),
        ],
        compiler_params=pltpu.CompilerParams(
            collective_id=0, has_side_effects=True, vmem_limit_bytes=56 * 2**20
        ),
        name="front",
    )(hidden, seg_rim, tap_mask, depth, kernel, kernel_b, *vectors, *pairs, *shards, outer)
PACK_A = 1280
PACK_B = 768
SMALL_AT = 1152


def chips_of(me, size):
    core = lax.rem(me, 2)
    count = size // 2
    index = lax.div(me, 2)
    return index, count, lambda other: other * 2 + core


def pair_of(me, size):
    index = lax.rem(lax.div(me, 2), 2)
    return index, 2, lambda other: flip(me, 2)


def column_of(me, size):
    index = lax.div(me, TEAM)
    rest = lax.rem(me, TEAM)
    return index, size // TEAM, lambda other: other * TEAM + rest


def part_rows(base, count):
    return pl.ds(pl.multiple_of(base, 16), count)


def others(index, count):
    return [lax.rem(index + o, count) for o in range(1, count)]


def scatter_copies(stage, me, size, staged, came, send, recv):
    index, count, device = stage(me, size)
    piece = staged.shape[0] // count
    return [
        remote(staged.at[part_rows(other * piece, piece), :], came.at[index], send.at[other],
               recv.at[index], {"ctx": device(other)})
        for other in others(index, count)
    ]


def scatter_wait(stage, me, size, staged, came, send, recv):
    index, count, device = stage(me, size)
    piece = staged.shape[0] // count
    for other in others(index, count):
        remote(staged.at[part_rows(index * piece, piece), :], came.at[other], send.at[index],
               recv.at[other], {"ctx": device(other)}).wait_recv()


def share_copies(stage, me, size, fin, base, piece, send, recv):
    index, count, device = stage(me, size)
    view = fin.at[part_rows(base + index * piece, piece), :]
    return [
        remote(view, view, send.at[other], recv.at[index], {"ctx": device(other)})
        for other in others(index, count)
    ]


def share_wait(stage, me, size, fin, base, piece, send, recv):
    index, count, device = stage(me, size)
    for other in others(index, count):
        view = fin.at[part_rows(base + other * piece, piece), :]
        remote(view, view, send.at[index], recv.at[other], {"ctx": device(other)}).wait_recv()


def in_chunks(rows, body):
    chunk = max(c for c in range(16, 241, 16) if rows % c == 0)

    def step(i, carry):
        body(pl.multiple_of(i * chunk, 16), chunk)
        return carry

    lax.fori_loop(0, rows // chunk, step, 0)


def wide(value):
    return value.astype(jnp.float32)


def back_kernel(names, a_names, b_names, loaded, *refs):
    count_a, count_b = len(a_names), len(b_names)
    r = types.SimpleNamespace(**dict(zip(names, refs)))
    late = refs[len(names) :]
    block_a = types.SimpleNamespace(**dict(zip(a_names, late[:count_a])))
    block_b = types.SimpleNamespace(**dict(zip(b_names, late[count_a : count_a + count_b])))
    fetch_refs = late[count_a + count_b :]
    v = types.SimpleNamespace(**dict(zip(loaded, fetch_refs[len(loaded) :])))
    me, side = lax.axis_index("ctx"), lax.axis_index("wsh")
    size = lax.axis_size("ctx")
    core = lax.rem(me, 2)
    rank = lax.rem(me, TEAM)
    chip = lax.div(rank, 2)
    base = me - rank
    team = lax.div(me, TEAM)
    teams = size // TEAM
    twin, across = {"ctx": flip(me, 1)}, {"wsh": 1 - side}
    right, left = lax.rem(me + TEAM, size), lax.rem(me + size - TEAM, size)
    after, prior = lax.rem(me + 1, size), lax.rem(me + size - 1, size)
    seqs, block, model = v.x.shape
    width = HEADS * HEAD_DIM
    halo = (TEAM - 1) * block
    groups = model // LANES
    low = jnp.bfloat16
    index, count, device = chips_of(me, size)
    greet(
        [twin, across, {"ctx": base + mate(rank, 3)}, {"ctx": after}, {"ctx": prior}]
        + [{"ctx": device(other)} for other in others(index, count)]
    )

    def block_of(k):
        return pl.ds(pl.multiple_of(k * block, 16), block)

    def halo_left(c):
        return remote(r.window.at[block_of(2 * TEAM - 1 + c), :], r.from_left.at[block_of(c), :],
                      r.send_l.at[c], r.recv_l.at[c], {"ctx": right})

    def halo_right(c):
        return remote(r.window.at[block_of(c), :], r.from_right.at[block_of(c + 1), :],
                      r.send_r.at[c], r.recv_r.at[c], {"ctx": left})

    for k in range(TEAM - 1):
        to_right = halo_left(chip * k + (1 - chip) * (TEAM - 2 - k))
        to_left = halo_right(chip * k + (1 - chip) * ((k + 1) % (TEAM - 1)))
        pl.when(team < teams - 1)(to_right.start)
        pl.when(team > 0)(to_left.start)

    fetched = types.SimpleNamespace()
    for k, name in enumerate(loaded):
        copy = pltpu.make_async_copy(fetch_refs[k], fetch_refs[len(loaded) + k], r.load.at[k])
        setattr(fetched, name, copy)
    center = pltpu.make_async_copy(r.window.at[pl.ds(halo, TEAM * block), :], r.mine,
                                   r.load.at[len(loaded)])
    fetched.keep.start()
    fetched.came.start()
    center.start()

    def q_copy(o):
        other = mate(rank, o)
        return remote(r.dq.at[other], r.q_parts.at[rank], r.send_q.at[o], r.recv_q.at[o],
                      {"ctx": base + other})

    own_q = pltpu.make_async_copy(r.dq.at[rank], r.q_parts.at[rank], r.recv_q.at[0])
    for o in (3, 2, 1):
        q_copy(o).start()
    own_q.start()
    for name in loaded[2:]:
        getattr(fetched, name).start()

    def have(*copies):
        for copy in copies:
            copy.wait()

    half_ff = v.keep.shape[1]
    pair_index, _, _ = pair_of(me, size)
    have(fetched.keep, fetched.came)

    def stage_across(at, n):
        rows = part_rows(at, n)
        r.ff_send[rows, :] = (v.keep[1 - side, rows, :] + wide(v.came[1 - side, rows, :])).astype(low)
        v.keep[side, rows, :] = v.keep[side, rows, :] + wide(v.came[side, rows, :])

    in_chunks(half_ff, stage_across)
    ff_across = remote(r.ff_send, r.ff_came, r.send_p.at[0], r.recv_p.at[0], across)
    ff_across.start()

    small = r.sums
    small[...] = jnp.zeros_like(small)
    for j in range(KERNEL):
        row = lax.broadcasted_iota(jnp.int32, (2 * LANES, width), 0)
        col = lax.broadcasted_iota(jnp.int32, (2 * LANES, width), 1)
        row = jnp.where(row >= LANES, row - LANES, row)
        r.spread[j] = jnp.where(row == 8 * j + col // HEAD_DIM, 1.0, 0.0).astype(low)

    zero_block = jnp.zeros((block, width), low)
    r.from_left[pl.ds((TEAM - 1) * block, block), :] = zero_block
    r.from_right[0:block, :] = zero_block

    @pl.when(team == 0)
    def _():
        for k in range(TEAM - 1):
            r.from_left[pl.ds(k * block, block), :] = zero_block

    @pl.when(team == teams - 1)
    def _():
        for k in range(1, TEAM):
            r.from_right[pl.ds(k * block, block), :] = zero_block

    @pl.when(me == 0)
    def _():
        r.dd_low[...] = jnp.zeros_like(r.dd_low)
        r.rim_low[...] = jnp.zeros_like(r.rim_low)

    @pl.when(me == size - 1)
    def _():
        r.dd_high[...] = jnp.zeros_like(r.dd_high)
        r.rim_high[...] = jnp.zeros_like(r.rim_high)

    small_ref = r.small
    kernel_w = kernel_rows(
        wide(small_ref[ROW_IN_KERNEL_W : ROW_IN_KERNEL_W + TAP_ROWS, :]),
        wide(small_ref[SMALL_IN + ROW_IN_KERNEL_W : SMALL_IN + ROW_IN_KERNEL_W + TAP_ROWS, :]),
    )
    lead = RIM - KERNEL // 2
    chunk = 128
    r.d_ext[...] = jnp.zeros_like(r.d_ext)
    have(fetched.dconv, fetched.ext, fetched.kern, fetched.point, fetched.queries, fetched.spans)
    wide_ref, tall_ref = r.wide, r.tall

    def conv_back(s):
        r.seg_col[s] = jnp.broadcast_to(r.seg[s : s + 1, :], (LANES, r.seg.shape[1])).T
        for j in range(KERNEL):
            wide_ref[8 * j : 8 * j + 8, :] = (
                v.kern[s, 8 * j : 8 * j + 8, :] * r.mask[s, j : j + 1, :]
            )
        wide_ref[TAP_ROWS:, :] = jnp.zeros((LANES - TAP_ROWS, block), jnp.float32)
        tall = wide_ref[...].T
        high = tall.astype(low)
        both = jnp.concatenate([high, (tall - wide(high)).astype(low)], axis=1)
        for c in range(block // chunk):
            rows = slice(c * chunk, (c + 1) * chunk)
            grad = wide(v.dconv[s, rows, :])
            taps = jnp.zeros((chunk, LANES), jnp.float32)
            for j in range(KERNEL):
                near = jnp.concatenate(
                    [v.ext[s, g, pl.ds(lead + j + c * chunk, chunk), :] for g in range(3)],
                    axis=1,
                )
                term = near * grad
                first = term.astype(low)
                second = (term - wide(first)).astype(low)
                taps = taps + rows_nt(first, r.spread[j, 0:LANES, :])
                taps = taps + rows_nt(second, r.spread[j, 0:LANES, :])
                weight = dot(both[rows, :], r.spread[j]) * grad
                for g in range(3):
                    r.d_ext[s, g, pl.ds(lead + j + c * chunk, chunk), :] += weight[
                        :, lane_group(g)
                    ]
            tall_ref[rows, :] = taps
        back = tall_ref[...].T
        inner = jnp.zeros((8, block), jnp.float32)
        for j in range(KERNEL):
            inner = inner + v.kern[s, 8 * j : 8 * j + 8, :] * (
                back[8 * j : 8 * j + 8, :] * r.mask[s, j : j + 1, :]
            )
        for j in range(KERNEL):
            wide_ref[8 * j : 8 * j + 8, :] = v.kern[s, 8 * j : 8 * j + 8, :] * (
                back[8 * j : 8 * j + 8, :] * r.mask[s, j : j + 1, :] - inner
            )
        d_logits = wide_ref[0:TAP_ROWS, :].astype(low)
        mixed = (v.spans[s] * wide(v.queries[s])).astype(low)
        kernel_grad = dot(d_logits, mixed)
        kernel_bias = dot(d_logits, jnp.ones((block, LANES), low))
        for w in range(2):
            small[w, ROW_KERNEL_W : ROW_KERNEL_W + TAP_ROWS, :] += kernel_grad
            for g in range(3):
                small[w, ROW_KERNEL_B : ROW_KERNEL_B + 24, lane_group(g)] += kernel_bias[
                    24 * g : 24 * g + 24, :
                ]
        d_mixed = dot(wide_ref[...].T.astype(low), kernel_w)
        d_spans = (d_mixed * wide(v.queries[s])).astype(low)
        v.spans[s] = d_mixed * v.spans[s]
        v.dconv[s] = d_spans
        bias = jnp.sum(wide(d_spans), axis=0, keepdims=True)
        for w in range(2):
            small[w, ROW_POINT_B : ROW_POINT_B + 1, :] += bias
        d_depth = rows_nt(d_spans, v.point[...])
        for g in range(groups):
            r.dd[s, g, pl.ds(RIM, block), :] = d_depth[:, lane_group(g)]
        r.dd_first[s] = d_depth[0:RIM, :].astype(low)
        r.dd_last[s] = d_depth[block - RIM : block, :].astype(low)
        for g in range(3):
            r.rim_first[s, :, lane_group(g)] = r.d_ext[s, g, 0:RIM, :].astype(low)
            r.rim_last[s, :, lane_group(g)] = r.d_ext[
                s, g, RIM + block : 2 * RIM + block, :
            ].astype(low)


    def kv_copy(k):
        return (
            pltpu.make_async_copy(r.mine.at[block_of(k), :], r.kv_parts.at[rank], r.recv_kv.at[rank]),
            remote(r.mine.at[block_of(k), :], r.kv_parts.at[rank], r.send_kv.at[k],
                   r.recv_kv.at[rank], {"ctx": base + k}),
        )

    def return_block(k):
        pl.when((k <= TEAM - 2) & (team > 0))(lambda: halo_left(lax.rem(k, TEAM - 1)).wait_recv())
        pl.when((k >= 1) & (team < teams - 1))(
            lambda: halo_right(lax.rem(k + TEAM - 2, TEAM - 1)).wait_recv()
        )
        rows = block_of(k)
        r.mine[rows, :] = (
            wide(r.mine[rows, :]) + wide(r.from_left[rows, :]) + wide(r.from_right[rows, :])
        ).astype(low)
        pair = kv_copy(k)
        pl.when(k == rank)(pair[0].start)
        pl.when(k != rank)(pair[1].start)


    ff_base = core * (2 * half_ff) + pair_index * half_ff
    column_index, column_count, _ = column_of(me, size)
    column_piece = half_ff // column_count
    column_args = (column_of, me, size, r.ff_send, r.ff_column, r.send_c, r.recv_c)
    column_share = (column_of, me, size, r.fin_ff, ff_base, column_piece, r.send_cg, r.recv_cg)

    def piece_copy(fin, start, pair_rows, rows, k, mine, send, recv):
        side_of_pair = pair_index if mine else 1 - pair_index
        view = fin.at[part_rows(start + side_of_pair * pair_rows + k * rows, rows), :]
        return remote(view, view, send.at[k], recv.at[k], {"ctx": flip(me, 2)})

    def ff_piece(k, mine):
        return piece_copy(r.fin_ff, core * (2 * half_ff), half_ff, column_piece, k, mine,
                          r.send_pg, r.recv_pg)

    def wait_piece(spec, other):
        stage, _, _, fin, start, rows, send, recv = spec
        place, _, device_of = stage(me, size)
        view = fin.at[part_rows(start + other * rows, rows), :]
        remote(view, view, send.at[place], recv.at[other], {"ctx": device_of(other)}).wait_recv()

    def ff_to_column():
        ff_across.wait()

        def body(at, n):
            rows = part_rows(at, n)
            value = v.keep[side, rows, :] + wide(r.ff_came[rows, :])
            v.keep[side, rows, :] = value
            r.ff_send[rows, :] = value.astype(low)

        in_chunks(half_ff, body)
        for copy in scatter_copies(*column_args):
            copy.start()

    def ff_to_share():
        scatter_wait(*column_args)
        rows = part_rows(column_index * column_piece, column_piece)
        total = v.keep[side, rows, :]
        for other in others(column_index, column_count):
            total = total + wide(r.ff_column[other])
        r.ff_send[rows, :] = total.astype(low)
        own = pltpu.make_async_copy(
            r.ff_send.at[rows, :],
            r.fin_ff.at[part_rows(ff_base + column_index * column_piece, column_piece), :],
            r.load.at[0],
        )
        own.start()
        own.wait()
        for copy in share_copies(*column_share):
            copy.start()
        ff_piece(column_index, True).start()

    def ff_to_pair():
        for other in others(column_index, column_count):
            wait_piece(column_share, other)
            ff_piece(other, True).start()

    def ff_twin():
        view = r.fin_ff.at[part_rows(core * (2 * half_ff), 2 * half_ff), :]
        return remote(view, view, r.send_pg.at[column_count], r.recv_pg.at[column_count], twin)

    def ff_to_twin():
        for k in range(column_count):
            ff_piece(k, False).wait_recv()
        ff_twin().start()


    conv_back(0)
    center.wait()
    there = (1 - chip) * (TEAM // 2)
    here = chip * (TEAM // 2)
    return_block(there)
    conv_back(1)
    rims = [
        (remote(r.dd_last, r.dd_low, r.send_h.at[0], r.recv_h.at[0], {"ctx": after}), 1),
        (remote(r.rim_last, r.rim_low, r.send_h.at[1], r.recv_h.at[1], {"ctx": after}), 1),
        (remote(r.dd_first, r.dd_high, r.send_h.at[2], r.recv_h.at[2], {"ctx": prior}), 0),
        (remote(r.rim_first, r.rim_high, r.send_h.at[3], r.recv_h.at[3], {"ctx": prior}), 0),
    ]
    for copy, forward in rims:
        pl.when(me < size - 1 if forward else me > 0)(copy.start)

    return_block(there + 1)
    ff_to_column()
    have(fetched.depth, fetched.xrim)
    strip = 32

    def flat_rows(ref):
        return ref[...].reshape(seqs * block, ref.shape[2])

    point_grad = dot_tn(flat_rows(v.depth), flat_rows(v.dconv)).astype(low)
    for w in range(2):
        block_a.pack[w, 0:width, :] = point_grad[w * width : (w + 1) * width, :]
    for g in range(groups):
        def tap_step(c, sums, g=g):
            out = list(sums)
            for s in range(seqs):
                start = c * strip
                here = r.seg_col[s, pl.ds(RIM + start, strip), :]
                grad = r.dd[s, g, pl.ds(RIM + start, strip), :]
                for j in range(KERNEL):
                    same = r.seg_col[s, pl.ds(lead + j + start, strip), :] == here
                    near = v.xrim[s, g, pl.ds(lead + j + start, strip), :]
                    out[j] = out[j] + fold_rows(jnp.where(same, near, 0.0) * grad)
            return tuple(out)

        sums = lax.fori_loop(
            0, block // strip, tap_step,
            tuple(jnp.zeros((8, LANES), jnp.float32) for _ in range(KERNEL)),
        )
        for j in range(KERNEL):
            small[g // 3, j : j + 1, lane_group(g % 3)] = jnp.sum(sums[j], axis=0, keepdims=True)

    return_block(here + 1 - chip)
    return_block(here + chip)
    have(fetched.convw, fetched.x)
    for copy, forward in rims:
        pl.when(me > 0 if forward else me < size - 1)(copy.wait_recv)
    near_taps = KERNEL // 2
    for s in range(seqs):
        for g in range(3):
            head = pl.ds(RIM, RIM)
            tail = pl.ds(block, RIM)
            r.d_ext[s, g, head, :] += wide(r.rim_low[s, :, lane_group(g)])
            r.d_ext[s, g, tail, :] += wide(r.rim_high[s, :, lane_group(g)])
            v.queries[s, :, lane_group(g)] = r.d_ext[s, g, pl.ds(RIM, block), :].astype(low)
        for g in range(groups):
            r.dd[s, g, 0:RIM, :] = wide(r.dd_low[s, :, lane_group(g)])
            r.dd[s, g, pl.ds(RIM + block, RIM), :] = wide(r.dd_high[s, :, lane_group(g)])
        bias = jnp.sum(wide(v.queries[s]), axis=0, keepdims=True)
        for w in range(2):
            small[w, ROW_CONV_B : ROW_CONV_B + 1, :] += bias
    conv_grad = dot_tn(flat_rows(v.x), flat_rows(v.queries)).astype(low)
    for w in range(2):
        block_a.pack[w, width : 2 * width, :] = conv_grad[w * width : (w + 1) * width, :]

    def core_copy(blk):
        pack = blk.pack
        half = pack.shape[1] // 2
        return remote(pack.at[:, part_rows((1 - core) * half, half), :], blk.twin,
                      blk.send_core.at[0], blk.recv_core.at[0], twin)

    def y_copy(blk):
        return remote(blk.ysend, blk.ycame, blk.send_core.at[1],
                      blk.recv_core.at[1], across)

    def core_done(blk):
        core_copy(blk).wait()
        pack, came = blk.pack, blk.twin
        half = pack.shape[1] // 2

        def body(at, n):
            rows, there = part_rows(at, n), part_rows(core * half + at, n)
            blk.ysend[rows, :] = (
                wide(pack[1 - side, there, :]) + wide(came[1 - side, rows, :])
            ).astype(low)
            blk.acc[rows, :] = wide(pack[side, there, :]) + wide(came[side, rows, :])

        in_chunks(half, body)
        y_copy(blk).start()

    def chips_args(blk):
        return (chips_of, me, size, blk.ysend, blk.chips,
                blk.send_s, blk.recv_s)

    def y_done(blk):
        y_copy(blk).wait()

        def body(at, n):
            rows = part_rows(at, n)
            value = blk.acc[rows, :] + wide(blk.ycame[rows, :])
            blk.acc[rows, :] = value
            blk.ysend[rows, :] = value.astype(low)

        in_chunks(blk.ysend.shape[0], body)
        for copy in scatter_copies(*chips_args(blk)):
            copy.start()

    def pair_copy_a():
        rows = block_a.ysend.shape[0] // 2
        return remote(block_a.ysend.at[part_rows((1 - pair_index) * rows, rows), :], block_a.pair,
                      block_a.send_core.at[3], block_a.recv_core.at[3], {"ctx": flip(me, 2)})

    def y_done_a():
        y_copy(block_a).wait()

        def body(at, n):
            rows = part_rows(at, n)
            value = block_a.acc[rows, :] + wide(block_a.ycame[rows, :])
            block_a.acc[rows, :] = value
            block_a.ysend[rows, :] = value.astype(low)

        in_chunks(block_a.ysend.shape[0], body)
        pair_copy_a().start()

    def column_args_a():
        rows = block_a.ysend.shape[0] // 2
        return (column_of, me, size, block_a.ysend.at[pl.ds(0, rows), :], block_a.column,
                block_a.send_s, block_a.recv_s)

    def pair_done_a():
        pair_copy_a().wait()
        half = block_a.ysend.shape[0] // 2

        def body(at, n):
            rows = part_rows(at, n)
            value = block_a.acc[part_rows(pair_index * half + at, n), :] + wide(
                block_a.pair[rows, :]
            )
            block_a.acc[rows, :] = value
            block_a.ysend[rows, :] = value.astype(low)

        in_chunks(half, body)
        for copy in scatter_copies(*column_args_a()):
            copy.start()

    def column_share_a():
        half = block_a.ysend.shape[0]
        return (column_of, me, size, block_a.fin, core * half + pair_index * (half // 2),
                half // 2 // (size // TEAM), block_a.send_g, block_a.recv_g)

    def piece_a(k, mine):
        half = block_a.ysend.shape[0]
        return piece_copy(block_a.fin, core * half, half // 2, half // 2 // column_count, k, mine,
                          block_a.send_p, block_a.recv_p)

    def column_done_a():
        scatter_wait(*column_args_a())
        place, number, _ = column_of(me, size)
        half = block_a.ysend.shape[0]
        piece_rows = half // 2 // number
        value = block_a.acc[part_rows(place * piece_rows, piece_rows), :]
        for other in others(place, number):
            value = value + wide(block_a.column[other])
        at = core * half + pair_index * (half // 2) + place * piece_rows
        block_a.fin[part_rows(at, piece_rows), :] = value.astype(low)
        for copy in share_copies(*column_share_a()):
            copy.start()
        piece_a(column_index, True).start()

    def share_done_a():
        for other in others(column_index, column_count):
            wait_piece(column_share_a(), other)
            piece_a(other, True).start()

    def last_done_a():
        for k in range(column_count):
            piece_a(k, False).wait_recv()
        twin_copy(block_a).start()

    def finish_a():
        for copy in scatter_copies(*column_args_a()):
            copy.wait_send()
        for copy in share_copies(*column_share_a()):
            copy.wait_send()
        for k in range(column_count):
            piece_a(k, True).wait_send()
        twin_copy(block_a).wait()

    def share_args(blk):
        half = blk.ysend.shape[0]
        return (chips_of, me, size, blk.fin, core * half, half // count,
                blk.send_g, blk.recv_g)

    def chips_done(blk):
        scatter_wait(*chips_args(blk))
        half = blk.ysend.shape[0]
        piece = half // count
        value = blk.acc[part_rows(index * piece, piece), :]
        for other in others(index, count):
            value = value + wide(blk.chips[other])
        blk.fin[part_rows(core * half + index * piece, piece), :] = value.astype(low)
        for copy in share_copies(*share_args(blk)):
            copy.start()

    def twin_copy(blk):
        fin = blk.fin
        half = fin.shape[0] // 2
        view = fin.at[part_rows(core * half, half), :]
        return remote(view, view, blk.send_core.at[2], blk.recv_core.at[2], twin)

    def share_done(blk):
        share_wait(*share_args(blk))
        twin_copy(blk).start()

    def finish(blk):
        for copy in scatter_copies(*chips_args(blk)):
            copy.wait_send()
        for copy in share_copies(*share_args(blk)):
            copy.wait_send()
        twin_copy(blk).wait()

    own_q.wait()
    for o in range(1, TEAM):
        q_copy(o).wait_send()
        remote(r.dq.at[rank], r.q_parts.at[mate(rank, o)], r.send_q.at[o], r.recv_q.at[o],
               {"ctx": base + mate(rank, o)}).wait_recv()
    for s in range(seqs):
        one, two = r.q_parts.at[2 * s], r.q_parts.at[2 * s + 1]
        queries = (
            one[:, lane_group(0)],
            mixed_lanes(wide(one[:, lane_group(1)]), half_turn(wide(two[:, lane_group(1)]))),
            two[:, lane_group(0)],
        )
        for g in range(3):
            r.d_cat[s, :, lane_group(6 + g)] = (
                wide(queries[g]) + v.spans[s, :, lane_group(g)]
            ).astype(low)
    for s in range(seqs):
        bias = jnp.sum(wide(r.d_cat[s, :, 2 * width :]), axis=0, keepdims=True)
        for w in range(2):
            small[w, ROW_QUERY_B : ROW_QUERY_B + 1, :] += bias
    query_grad = dot_tn(
        flat_rows(v.x), r.d_cat[:, :, 2 * width :].reshape(seqs * block, width)
    ).astype(low)
    for w in range(2):
        block_a.pack[w, 2 * width : 3 * width, :] = query_grad[w * width : (w + 1) * width, :]
    for k, row in enumerate((ROW_GAIN2, ROW_SHIFT2, ROW_OUTER_B, ROW_GAIN1, ROW_SHIFT1, ROW_OUTPUT_B)):
        for w in range(2):
            small[w, row : row + 1, :] = r.vec[k : k + 1, w * 384 : (w + 1) * 384]
    for w in range(2):
        for k in range(4):
            at = (4 * w + k) * 384
            small[w, ROW_INNER_B + k : ROW_INNER_B + k + 1, :] = r.bias[0:1, at : at + 384]

    upper = lax.rem(rank, 2) == 1
    heads = jnp.sum(wide(r.mine[...]), axis=0, keepdims=True)
    heads = jnp.broadcast_to(heads, (8, width))
    middle, outer_pair = heads[:, lane_group(1)], heads[:, lane_group(2)]
    none = jnp.zeros_like(middle)
    bias = (
        jnp.where(upper, none, outer_pair),
        jnp.where(upper, mixed_lanes(none, middle), mixed_lanes(half_turn(middle), none)),
        jnp.where(upper, outer_pair, none),
    )
    for w in range(2):
        for g in range(3):
            small[w, ROW_VALUE_B : ROW_VALUE_B + 1, lane_group(g)] = bias[g][0:1, :]
    for w in range(2):
        block_a.pack[w, SMALL_AT : SMALL_AT + SMALL_ROWS, :] = small[w].astype(low)
    core_copy(block_a).start()
    core_done(block_a)
    ff_to_share()
    for k in range(TEAM):
        pl.when(k == rank)(kv_copy(k)[0].wait)
        pl.when(k != rank)(kv_copy(k)[1].wait_send)
    for o in range(1, TEAM):
        other = mate(rank, o)
        remote(r.mine.at[block_of(rank), :], r.kv_parts.at[other], r.send_kv.at[rank],
               r.recv_kv.at[other], {"ctx": base + other}).wait_recv()
    for s in range(seqs):
        one, two = r.kv_parts.at[2 * s], r.kv_parts.at[2 * s + 1]
        mid_one, mid_two = wide(one[:, lane_group(1)]), wide(two[:, lane_group(1)])
        r.d_cat[s, :, lane_group(0)] = one[:, lane_group(0)]
        r.d_cat[s, :, lane_group(1)] = mixed_lanes(mid_one, half_turn(mid_two)).astype(low)
        r.d_cat[s, :, lane_group(2)] = two[:, lane_group(0)]
        r.d_cat[s, :, lane_group(3)] = one[:, lane_group(2)]
        r.d_cat[s, :, lane_group(4)] = mixed_lanes(half_turn(mid_one), mid_two).astype(low)
        r.d_cat[s, :, lane_group(5)] = two[:, lane_group(2)]
    grads = r.d_cat[:, :, 0 : 2 * width].reshape(seqs * block, 2 * width)
    for w in range(2):
        piece = dot_tn(
            v.x[:, :, w * width : (w + 1) * width].reshape(seqs * block, width), grads
        ).astype(low)
        for k in range(2):
            block_b.pack[w, k * width : (k + 1) * width, :] = piece[:, k * width : (k + 1) * width]
    core_copy(block_b).start()
    core_done(block_b)
    y_done_a()
    have(fetched.ds, fetched.key, fetched.value, fetched.query)
    def taps_row(j, g):
        return wide(small_ref[(g // 3) * SMALL_IN + j : (g // 3) * SMALL_IN + j + 1,
                              lane_group(g % 3)])

    def depth_strip(c, s):
        start = c * strip
        here = r.seg_col[s, pl.ds(RIM + start, strip), :]
        rows = pl.ds(pl.multiple_of(start, strip), strip)
        sums = [v.ds[s, rows, lane_group(g)] for g in range(groups)]
        for j in range(KERNEL):
            same = r.seg_col[s, pl.ds(RIM + near_taps - j + start, strip), :] == here
            for g in range(groups):
                near = r.dd[s, g, pl.ds(RIM + near_taps - j + start, strip), :]
                sums[g] = sums[g] + jnp.where(same, near, 0.0) * taps_row(j, g)
        for g in range(groups):
            v.ds[s, rows, lane_group(g)] = sums[g]
        return s

    for s in range(seqs):
        lax.fori_loop(0, block // strip, depth_strip, s)
    pair_done_a()
    y_done(block_b)
    ff_to_pair()
    column_done_a()
    for s in range(seqs):
        v.ds[s] += (
            rows_nt(v.queries[s], v.convw[...])
            + rows_nt(r.d_cat[s, :, 0:width], v.key[...])
            + rows_nt(r.d_cat[s, :, width : 2 * width], v.value[...])
            + rows_nt(r.d_cat[s, :, 2 * width :], v.query[...])
        )
    out_copy = pltpu.make_async_copy(v.ds, r.input_grad, r.load.at[1])
    out_copy.start()
    ff_to_twin()
    chips_done(block_b)
    share_done_a()
    last_done_a()
    share_done(block_b)
    finish_a()
    finish(block_b)
    ff_twin().wait()
    for copy in scatter_copies(*column_args):
        copy.wait_send()
    for copy in share_copies(*column_share):
        copy.wait_send()
    for k in range(column_count):
        ff_piece(k, True).wait_send()
    for copy, forward in rims:
        pl.when(me < size - 1 if forward else me > 0)(copy.wait_send)
    for k in range(TEAM - 1):
        pl.when(team < teams - 1)(halo_left(k).wait_send)
        pl.when(team > 0)(halo_right(k).wait_send)
    out_copy.wait()


def padded(rows, unit):
    return -(-rows // unit) * unit


def back(held, window, dq_parts, loaded):
    size = lax.axis_size("ctx")
    unit = 16 * size
    seqs, block, model = loaded["x"].shape
    width = HEADS * HEAD_DIM
    halo = (TEAM - 1) * block
    span = block + 2 * RIM
    chips, column = size // 2, size // TEAM
    low, full = jnp.bfloat16, jnp.float32
    dma = pltpu.SemaphoreType.DMA
    half_ff = loaded["keep"].shape[1]
    outs = dict(
        input_grad=jax.ShapeDtypeStruct((seqs, block, model), full),
        fin_ff=jax.ShapeDtypeStruct((4 * half_ff, width), low),
    )
    scratch = dict(
        mine=pltpu.VMEM((TEAM * block, width), low),
        from_right=pltpu.VMEM((TEAM * block, width), low),
        from_left=pltpu.VMEM((TEAM * block, width), low),
        kv_parts=pltpu.VMEM((TEAM, block, width), low),
        q_parts=pltpu.VMEM((TEAM, block, 2 * LANES), low),
        ff_send=pltpu.VMEM((half_ff, width), low),
        ff_came=pltpu.VMEM((half_ff, width), low),
        ff_column=pltpu.VMEM((column, half_ff // column, width), low),
        spread=pltpu.VMEM((KERNEL, 2 * LANES, width), low),
        sums=pltpu.VMEM((2, SMALL_ROWS, width), full),
        wide=pltpu.VMEM((LANES, block), full),
        tall=pltpu.VMEM((block, LANES), full),
        seg_col=pltpu.VMEM((seqs, held["seg"].shape[1], LANES), full),
        d_ext=pltpu.VMEM((seqs, 3, span, LANES), full),
        dd=pltpu.VMEM((seqs, model // LANES, span, LANES), full),
        d_cat=pltpu.VMEM((seqs, block, 3 * width), low),
        dd_first=pltpu.VMEM((seqs, RIM, model), low),
        dd_last=pltpu.VMEM((seqs, RIM, model), low),
        dd_low=pltpu.VMEM((seqs, RIM, model), low),
        dd_high=pltpu.VMEM((seqs, RIM, model), low),
        rim_first=pltpu.VMEM((seqs, RIM, width), low),
        rim_last=pltpu.VMEM((seqs, RIM, width), low),
        rim_low=pltpu.VMEM((seqs, RIM, width), low),
        rim_high=pltpu.VMEM((seqs, RIM, width), low),
        send_l=dma((TEAM,)), recv_l=dma((TEAM,)), send_r=dma((TEAM,)), recv_r=dma((TEAM,)),
        send_q=dma((TEAM,)), recv_q=dma((TEAM,)), send_kv=dma((TEAM,)), recv_kv=dma((TEAM,)),
        send_h=dma((4,)), recv_h=dma((4,)), send_p=dma((1,)), recv_p=dma((1,)),
        send_c=dma((column,)), recv_c=dma((column,)), send_cg=dma((column,)),
        recv_cg=dma((column,)), send_pg=dma((column + 1,)),
        recv_pg=dma((column + 1,)),
        load=dma((len(loaded) + 1,)),
    )

    def block_scratch(rows):
        rows = padded(rows, unit)
        return dict(
            pack=pltpu.VMEM((2, rows, width), low),
            twin=pltpu.VMEM((2, rows // 2, width), low),
            ysend=pltpu.VMEM((rows // 2, width), low),
            ycame=pltpu.VMEM((rows // 2, width), low),
            acc=pltpu.VMEM((rows // 2, width), full),
            chips=pltpu.VMEM((chips, rows // 2 // chips, width), low),
            fin=pltpu.VMEM((rows, width), low),
            send_s=dma((chips,)), recv_s=dma((chips,)), send_g=dma((chips,)),
            recv_g=dma((chips,)), send_core=dma((4,)), recv_core=dma((4,)),
        )

    a_scratch, b_scratch = block_scratch(PACK_A), block_scratch(PACK_B)
    quarter = padded(PACK_A, unit) // 4
    del a_scratch["chips"]
    a_scratch.update(
        pair=pltpu.VMEM((quarter, width), low),
        column=pltpu.VMEM((column, quarter // column, width), low),
        send_p=dma((column,)), recv_p=dma((column,)),
    )
    del a_scratch["fin"], b_scratch["fin"]
    fin_shapes = [jax.ShapeDtypeStruct((padded(n, unit), width), low) for n in (PACK_A, PACK_B)]
    vmem = pl.BlockSpec(memory_space=pltpu.VMEM)
    anywhere = pl.BlockSpec(memory_space=pl.ANY)
    names = tuple(held) + ("window", "dq") + tuple(outs) + tuple(scratch)
    total_in = len(held) + 2
    fetch_count = len(loaded)

    def kernel(*refs):
        ins, loads = refs[:total_in], refs[total_in : total_in + fetch_count]
        at = total_in + fetch_count
        results = refs[at : at + len(outs)]
        fin_a, fin_b = refs[at + len(outs) : at + len(outs) + 2]
        late = refs[at + len(outs) + 2 :]
        first, late = late[: len(scratch)], late[len(scratch) :]
        a_refs, late = late[: len(a_scratch)], late[len(a_scratch) :]
        b_refs, holds = late[: len(b_scratch)], late[len(b_scratch) :]
        back_kernel(
            names, tuple(a_scratch) + ("fin",), tuple(b_scratch) + ("fin",), tuple(loaded),
            *ins, *results, *first, *a_refs, fin_a, *b_refs, fin_b, *loads, *holds,
        )

    holds = [pltpu.VMEM(a.shape, a.dtype) for a in loaded.values()]
    return pl.pallas_call(
        kernel,
        out_shape=list(outs.values()) + fin_shapes,
        in_specs=[vmem] * len(held) + [anywhere] * (2 + len(loaded)),
        out_specs=[anywhere] * 2 + [vmem] * 2,
        scratch_shapes=list(scratch.values()) + list(a_scratch.values())
        + list(b_scratch.values()) + holds,
        compiler_params=pltpu.CompilerParams(
            collective_id=5, has_side_effects=True, vmem_limit_bytes=65400 * 2**10
        ),
        name="back",
    )(*held.values(), window, dq_parts, *loaded.values())


STEP = 256
FF_CHUNK = 512
PACK_FF = 3840


def gelu_pair(value):
    share = 0.5 + 0.5 * lax.erf(value * 0.7071067811865476)
    bell = jnp.exp(-0.5 * value * value)
    return value * share, share + value * bell * 0.3989422804014327


def fold_rows(block):
    return jnp.sum(block.reshape(block.shape[0] // 8, 8, block.shape[1]), axis=0)


def norm_parts(value):
    center = value - jnp.mean(value, axis=-1, keepdims=True)
    spread = jnp.mean(center * center, axis=-1, keepdims=True)
    scale = lax.rsqrt(spread + 1e-05)
    return center * scale, scale


def norm_back(grad, unit, scale):
    return scale * (
        grad
        - jnp.mean(grad, axis=-1, keepdims=True)
        - unit * jnp.mean(grad * unit, axis=-1, keepdims=True)
    )


def middle_kernel(att_ref, conv_ref, x_ref, small_ref, og_any, ow_any, iw_any, uw_any, uw_came,
                  out_any, ds_any, dc_any, team_ref, keep_ref, xsend_ref, vec_ref, bias_ref,
                  og_ref, ow_ref, iw_ref, uw_ref, out_ref, ds_ref, dc_ref,
                  pack_ref, twin_ref, pieces, parts, joined_ref, low_ref, act_ref, slope_ref, do_ref, di_ref, db_ref,
                  sums_ref, wide_sums, send_a, recv_a, send_g, recv_g, send_t, recv_t, load, store):
    me = lax.axis_index("ctx")
    rank = lax.rem(me, TEAM)
    base = me - rank
    seqs, block, model = x_ref.shape
    width = HEADS * HEAD_DIM
    greet([{"ctx": base + mate(rank, o)} for o in range(1, TEAM)])

    def piece_copy(r):
        return (
            pltpu.make_async_copy(att_ref.at[r], pieces.at[rank], recv_a.at[rank]),
            remote(att_ref.at[r], pieces.at[rank], send_a.at[r], recv_a.at[rank],
                   {"ctx": base + r}),
        )

    def team_copy(r):
        return (
            pltpu.make_async_copy(parts.at[r], team_ref.at[rank], recv_g.at[rank]),
            remote(parts.at[r], team_ref.at[rank], send_g.at[r], recv_g.at[rank],
                   {"ctx": base + r}),
        )

    core, side = lax.rem(me, 2), lax.axis_index("wsh")
    for o in (1, 3, 2):
        piece_copy(mate(rank, o))[1].start()
    piece_copy(rank)[0].start()
    rows_in = uw_came.shape[1]
    came_at = part_rows((1 - side) * (2 * rows_in) + core * rows_in, rows_in)
    loads = [
        pltpu.make_async_copy(ow_any, ow_ref, load.at[0]),
        pltpu.make_async_copy(iw_any, iw_ref, load.at[1]),
        pltpu.make_async_copy(
            uw_any, uw_ref.at[:, part_rows(side * (2 * rows_in), 2 * rows_in), :], load.at[2]
        ),
        pltpu.make_async_copy(uw_came, uw_ref.at[:, came_at, :], load.at[3]),
        pltpu.make_async_copy(og_any, og_ref, load.at[4]),
    ]
    for copy in loads:
        copy.start()
    outer_twin = remote(uw_came, uw_ref.at[:, came_at, :], send_t.at[1], recv_t.at[1],
                        {"ctx": flip(me, 1)})
    outer_twin.start()
    sums_ref[...] = jnp.zeros_like(sums_ref)
    wide_sums[...] = jnp.zeros_like(wide_sums)
    own = lax.div(rank, 2)
    steps = block // STEP

    def row(index):
        return jnp.concatenate(
            [small_ref[index : index + 1, :], small_ref[SMALL_IN + index : SMALL_IN + index + 1, :]],
            axis=1,
        ).astype(jnp.float32)

    def body(i, carry):
        s = lax.rem(own + lax.div(i, steps), seqs)
        start = pl.multiple_of(lax.rem(i, steps) * STEP, STEP)
        rows = pl.ds(start, STEP)
        flat = pl.ds(pl.multiple_of(s * block + start, STEP), STEP)

        @pl.when(i == 0)
        def _():
            piece_copy(rank)[0].wait()
            remote(att_ref.at[rank], pieces.at[mate(rank, 1)], send_a.at[rank],
                   recv_a.at[mate(rank, 1)], {"ctx": base + mate(rank, 1)}).wait_recv()
            for copy in loads:
                copy.wait()
            outer_twin.wait()

        @pl.when(i == steps)
        def _():
            for o in (2, 3):
                remote(att_ref.at[rank], pieces.at[mate(rank, o)], send_a.at[rank],
                       recv_a.at[mate(rank, o)], {"ctx": base + mate(rank, o)}).wait_recv()

        first, second = pieces.at[2 * s], pieces.at[2 * s + 1]
        joined_ref[flat, lane_group(0)] = first[rows, lane_group(0)]
        joined_ref[flat, lane_group(1)] = mixed_lanes(
            first[rows, lane_group(1)].astype(jnp.float32),
            half_turn(second[rows, lane_group(1)].astype(jnp.float32)),
        ).astype(jnp.bfloat16)
        joined_ref[flat, lane_group(2)] = second[rows, lane_group(0)]
        joined_ref[flat, width:] = conv_ref[s, rows, :]
        branch = dot(joined_ref[flat, :], ow_ref[...]) + row(ROW_OUTPUT_B)
        unit1, scale1 = norm_parts(branch + x_ref[s, rows, :].astype(jnp.float32))
        gain1 = row(ROW_GAIN1)
        normed = unit1 * gain1 + row(ROW_SHIFT1)
        low_ref[flat, :] = normed.astype(jnp.bfloat16)
        outer = []
        part = model // GROUPS
        hidden = iw_ref.shape[2]
        for g in range(GROUPS):
            cols = slice(g * part, (g + 1) * part)
            for c in range(hidden // FF_CHUNK):
                span = slice(g * hidden + c * FF_CHUNK, g * hidden + (c + 1) * FF_CHUNK)
                near = slice(c * FF_CHUNK, (c + 1) * FF_CHUNK)
                bias = jnp.concatenate(
                    [
                        small_ref[
                            g * SMALL_IN + ROW_INNER_B + k // 3 : g * SMALL_IN + ROW_INNER_B + k // 3 + 1,
                            lane_group(k % 3),
                        ]
                        for k in range(c * FF_CHUNK // LANES, (c + 1) * FF_CHUNK // LANES)
                    ],
                    axis=1,
                ).astype(jnp.float32)
                inner = dot(low_ref[flat, cols], iw_ref[g, :, near]) + bias
                active, slope = gelu_pair(inner)
                act_ref[flat, span] = active.astype(jnp.bfloat16)
                slope_ref[:, span] = slope
            outer.append(dot(act_ref[flat, g * hidden : (g + 1) * hidden], uw_ref[g]))
        summed = jnp.concatenate(outer, axis=1) + row(ROW_OUTER_B) + normed
        unit2, scale2 = norm_parts(summed)
        gain2 = row(ROW_GAIN2)
        out_ref[s, rows, :] = (unit2 * gain2 + row(ROW_SHIFT2)).astype(jnp.bfloat16)
        grad = og_ref[s, rows, :].astype(jnp.float32)
        sums_ref[0] += fold_rows(grad * unit2)
        sums_ref[1] += fold_rows(grad)
        d_sum2 = norm_back(grad * gain2, unit2, scale2)
        d_outer = d_sum2.astype(jnp.bfloat16)
        do_ref[flat, :] = d_outer
        sums_ref[2] += fold_rows(d_outer.astype(jnp.float32))
        back = []
        for g in range(GROUPS):
            cols = slice(g * part, (g + 1) * part)
            for c in range(hidden // FF_CHUNK):
                span = slice(g * hidden + c * FF_CHUNK, g * hidden + (c + 1) * FF_CHUNK)
                near = slice(c * FF_CHUNK, (c + 1) * FF_CHUNK)
                d_inner = (
                    rows_nt(do_ref[flat, cols], uw_ref[g, near, :]) * slope_ref[:, span]
                ).astype(jnp.bfloat16)
                di_ref[flat, span] = d_inner
                wide_sums[:, span] += fold_rows(d_inner.astype(jnp.float32))
            back.append(rows_nt(di_ref[flat, g * hidden : (g + 1) * hidden], iw_ref[g]))
        d_normed = d_sum2 + jnp.concatenate(back, axis=1)
        sums_ref[3] += fold_rows(d_normed * unit1)
        sums_ref[4] += fold_rows(d_normed)
        d_sum1 = norm_back(d_normed * gain1, unit1, scale1)
        ds_ref[s, rows, :] = d_sum1
        d_branch = d_sum1.astype(jnp.bfloat16)
        db_ref[flat, :] = d_branch
        sums_ref[5] += fold_rows(d_branch.astype(jnp.float32))
        d_joined = rows_nt(d_branch, ow_ref[...])
        dc_ref[s, rows, :] = d_joined[:, width:].astype(jnp.bfloat16)
        parts[2 * s, rows, lane_group(0)] = d_joined[:, lane_group(0)].astype(jnp.bfloat16)
        parts[2 * s, rows, lane_group(1)] = half_turn(d_joined[:, lane_group(1)]).astype(
            jnp.bfloat16
        )
        parts[2 * s + 1, rows, lane_group(0)] = d_joined[:, lane_group(2)].astype(jnp.bfloat16)
        parts[2 * s + 1, rows, lane_group(1)] = d_joined[:, lane_group(1)].astype(jnp.bfloat16)

        @pl.when(i == steps - 1)
        def _():
            team_copy(rank)[0].start()
            team_copy(mate(rank, 1))[1].start()

        @pl.when(i == 2 * steps - 1)
        def _():
            team_copy(mate(rank, 2))[1].start()
            team_copy(mate(rank, 3))[1].start()

        return carry

    lax.fori_loop(0, seqs * steps, body, 0)
    stores = [
        pltpu.make_async_copy(out_ref, out_any, store.at[0]),
        pltpu.make_async_copy(ds_ref, ds_any, store.at[1]),
        pltpu.make_async_copy(dc_ref, dc_any, store.at[2]),
    ]
    for copy in stores:
        copy.start()

    half = width
    part = model // GROUPS
    hidden = iw_ref.shape[2]
    half_ff = pack_ref.shape[1] // 2
    early = half + part // 2 * (hidden // half)

    def exchange(at, rows, sem):
        return remote(
            pack_ref.at[:, part_rows((1 - core) * half_ff + at, rows), :],
            twin_ref.at[:, pl.ds(at, rows), :], send_t.at[sem], recv_t.at[sem],
            {"ctx": flip(me, 1)},
        )

    for w in range(2):
        for k in range(2):
            pack_ref[w, pl.ds(k * half_ff, half), :] = dot_tn(
                joined_ref[:, w * half : (w + 1) * half], db_ref[:, k * half : (k + 1) * half]
            ).astype(jnp.bfloat16)
    for g in range(GROUPS):
        for k in range(hidden // half):
            grads = dot_tn(
                low_ref[:, g * part : (g + 1) * part],
                di_ref[:, g * hidden + k * half : g * hidden + (k + 1) * half],
            ).astype(jnp.bfloat16)
            for w in range(2):
                pack_ref[w, pl.ds(g * half_ff + half + k * (part // 2), part // 2), :] = grads[
                    w * (part // 2) : (w + 1) * (part // 2), :
                ]
    exchange(0, early, 0).start()
    for g in range(GROUPS):
        for k in range(hidden // half):
            w, lower = k // 2, k % 2
            grads = dot_tn(
                act_ref[:, g * hidden + k * half : g * hidden + (k + 1) * half],
                do_ref[:, g * part : (g + 1) * part],
            ).astype(jnp.bfloat16)
            pack_ref[w, pl.ds(g * half_ff + early + lower * half, half), :] = grads
    exchange(early, half_ff - early, 2).start()
    for k in range(6):
        vec_ref[k : k + 1, :] = jnp.sum(sums_ref[k], axis=0, keepdims=True)
    vec_ref[6:, :] = jnp.zeros((2, model), jnp.float32)
    bias_ref[...] = jnp.broadcast_to(jnp.sum(wide_sums[...], axis=0, keepdims=True), bias_ref.shape)

    exchange(0, early, 0).wait()
    exchange(early, half_ff - early, 2).wait()
    pair_index, _, _ = pair_of(me, lax.axis_size("ctx"))
    quarter = half_ff // 2

    def add(at, n):
        here = part_rows(at, n)
        keep, give = pair_index * quarter, (1 - pair_index) * quarter
        for w in range(2):
            xsend_ref[w, here, :] = (
                wide(pack_ref[w, part_rows(core * half_ff + give + at, n), :])
                + wide(twin_ref[w, part_rows(give + at, n), :])
            ).astype(jnp.bfloat16)
            keep_ref[w, here, :] = wide(
                pack_ref[w, part_rows(core * half_ff + keep + at, n), :]
            ) + wide(twin_ref[w, part_rows(keep + at, n), :])

    in_chunks(quarter, add)
    team_copy(rank)[0].wait()
    for o in range(1, TEAM):
        other = mate(rank, o)
        piece_copy(other)[1].wait_send()
        team_copy(other)[1].wait_send()
        remote(parts.at[rank], team_ref.at[other], send_g.at[rank], recv_g.at[other],
               {"ctx": base + other}).wait_recv()
    for copy in stores:
        copy.wait()


def middle(attended, convolved, hidden, small, out_grad, output_w, inner_w, outer_w, outer_came):
    seqs, block, model = hidden.shape
    rows = seqs * block
    width = convolved.shape[2]
    inner = GROUPS * inner_w.shape[2]
    pack_rows = padded(PACK_FF, 16 * lax.axis_size("ctx"))
    vmem = pl.BlockSpec(memory_space=pltpu.VMEM)
    anywhere = pl.BlockSpec(memory_space=pl.ANY)
    low, full = jnp.bfloat16, jnp.float32
    dma = pltpu.SemaphoreType.DMA
    return pl.pallas_call(
        middle_kernel,
        out_shape=[
            jax.ShapeDtypeStruct((seqs, block, model), low),
            jax.ShapeDtypeStruct((seqs, block, model), full),
            jax.ShapeDtypeStruct((seqs, block, width), low),
            jax.ShapeDtypeStruct((TEAM, block, 2 * LANES), low),
            jax.ShapeDtypeStruct((2, pack_rows // 4, width), full),
            jax.ShapeDtypeStruct((2, pack_rows // 4, width), low),
            jax.ShapeDtypeStruct((8, model), full),
            jax.ShapeDtypeStruct((8, inner), full),
        ],
        in_specs=[anywhere] + [vmem] * 3 + [anywhere] * 5,
        out_specs=[anywhere] * 4 + [vmem] * 4,
        scratch_shapes=[
            pltpu.VMEM((seqs, block, model), low),
            pltpu.VMEM(output_w.shape, low),
            pltpu.VMEM(inner_w.shape, low),
            pltpu.VMEM((GROUPS, 2 * outer_w.shape[1], outer_w.shape[2]), low),
            pltpu.VMEM((seqs, block, model), low),
            pltpu.VMEM((seqs, block, model), full),
            pltpu.VMEM((seqs, block, width), low),
            pltpu.VMEM((2, pack_rows, width), low),
            pltpu.VMEM((2, pack_rows // 2, width), low),
            pltpu.VMEM((TEAM, block, 2 * LANES), low),
            pltpu.VMEM((TEAM, block, 2 * LANES), low),
            pltpu.VMEM((rows, model), low),
            pltpu.VMEM((rows, model), low),
            pltpu.VMEM((rows, inner), low),
            pltpu.VMEM((STEP, inner), full),
            pltpu.VMEM((rows, model), low),
            pltpu.VMEM((rows, inner), low),
            pltpu.VMEM((rows, model), low),
            pltpu.VMEM((6, 8, model), full),
            pltpu.VMEM((8, inner), full),
            dma((TEAM,)), dma((TEAM,)), dma((TEAM,)), dma((TEAM,)), dma((3,)), dma((3,)),
            dma((5,)), dma((3,)),
        ],
        compiler_params=pltpu.CompilerParams(
            collective_id=2, has_side_effects=True, vmem_limit_bytes=63 * 2**20
        ),
        name="middle",
    )(attended, convolved, hidden, small, out_grad, output_w, inner_w, outer_w, outer_came)


def finish_kernel(side_ref, ff_any, a_any, b_any, grad_any, out_any,
                  grad_out, out_out, query_out, key_out, value_out, point_out, conv_out,
                  output_out, inner_out, outer_out, depth_out, kernel_out, query_b, value_b, point_b, conv_b,
                  output_b, gain1, shift1, outer_b, gain2, shift2, inner_b, kernel_b,
                  ff, a, b, grad, out, wide_a, wide_b, wide_output, wide_inner, wide_outer,
                  load, store):
    width = HEADS * HEAD_DIM
    loads = [
        pltpu.make_async_copy(a_any.at[pl.ds(0, a.shape[0]), :], a, load.at[0]),
        pltpu.make_async_copy(b_any.at[pl.ds(0, b.shape[0]), :], b, load.at[1]),
        pltpu.make_async_copy(ff_any.at[pl.ds(0, ff.shape[0]), :], ff, load.at[2]),
        pltpu.make_async_copy(grad_any, grad, load.at[3]),
        pltpu.make_async_copy(out_any, out, load.at[4]),
    ]
    for copy in loads:
        copy.start()
    stores = []

    def put(src, dst):
        copy = pltpu.make_async_copy(src, dst, store.at[len(stores)])
        copy.start()
        stores.append(copy)

    loads[0].wait()
    for k, place in enumerate((point_out, conv_out, query_out)):
        rows = pl.ds(k * width, width)
        wide_a[rows, :] = a[rows, :].astype(jnp.float32)
        put(wide_a.at[rows, :], place)
    small = a[pl.ds(SMALL_AT, SMALL_ROWS), :].astype(jnp.float32)
    depth_out[...] = small[0:KERNEL, :]
    first = side_ref[0] == 0
    for ref, row in ((output_b, ROW_OUTPUT_B), (gain1, ROW_GAIN1), (shift1, ROW_SHIFT1),
                     (outer_b, ROW_OUTER_B), (gain2, ROW_GAIN2), (shift2, ROW_SHIFT2)):
        ref[...] = small[row : row + 1, :].reshape(width)
    inner_b[...] = jnp.concatenate(
        [small[ROW_INNER_B + k : ROW_INNER_B + k + 1, :] for k in range(4)], axis=1
    ).reshape(4 * width)
    block = small[16:24, :]
    turned = jnp.where(first, block, pltpu.roll(block, 192, axis=1))
    for ref, row in ((query_b, ROW_QUERY_B), (value_b, ROW_VALUE_B), (point_b, ROW_POINT_B),
                     (conv_b, ROW_CONV_B)):
        ref[...] = turned[row - 16 : row - 15, 0:192].reshape(192)
    taps = small[ROW_KERNEL_W : ROW_KERNEL_W + TAP_ROWS, :]
    half = jnp.where(first, taps, pltpu.roll(taps, 192, axis=1))[:, 0:192]
    pick = jnp.where(tap_major((TAP_ROWS, HEADS * KERNEL), 0), 1.0, 0.0)
    kernel_out[...] = dot_tn(pick.astype(jnp.bfloat16), half.astype(jnp.bfloat16))
    lanes = small[ROW_KERNEL_B : ROW_KERNEL_B + 24, :]
    column = jnp.concatenate([lanes[:, lane_group(g)] for g in range(3)], axis=0)
    wide_pick = jnp.where(
        first,
        jnp.where(tap_major((TAP_ROWS, LANES), 0), 1.0, 0.0),
        jnp.where(tap_major((TAP_ROWS, LANES), HEADS * KERNEL // 2), 1.0, 0.0),
    )
    count = HEADS * KERNEL // 2
    kernel_b[...] = jnp.sum(column * wide_pick, axis=0, keepdims=True)[:, 0:count].reshape(count)
    loads[1].wait()
    for k, place in enumerate((key_out, value_out)):
        rows = pl.ds(k * width, width)
        wide_b[rows, :] = b[rows, :].astype(jnp.float32)
        put(wide_b.at[rows, :], place)
    loads[2].wait()
    half_ff = ff.shape[0] // 2
    count = inner_out.shape[1]
    blocks = inner_out.shape[2] // width
    rows = outer_out.shape[1]
    for g in range(GROUPS):
        cols = slice(g * width, (g + 1) * width)
        wide_output[:, cols] = ff[pl.ds(g * half_ff, width), :].astype(jnp.float32)
        for k in range(blocks):
            at = g * half_ff + width + k * count
            wide_inner[g, :, k * width : (k + 1) * width] = ff[pl.ds(at, count), :].astype(
                jnp.float32
            )
        wide_outer[g] = ff[pl.ds(g * half_ff + width + blocks * count, rows), :].astype(
            jnp.float32
        )
    put(wide_output, output_out)
    put(wide_inner, inner_out)
    put(wide_outer, outer_out)
    loads[3].wait()
    put(grad, grad_out)
    loads[4].wait()
    put(out, out_out)
    for copy in stores:
        copy.wait()


def finish(side, fin_ff, fin_a, fin_b, grad_input, output, inner_shape, outer_shape):
    width = HEADS * HEAD_DIM
    full, low = jnp.float32, jnp.bfloat16
    anywhere = pl.BlockSpec(memory_space=pl.ANY)
    vmem = pl.BlockSpec(memory_space=pltpu.VMEM)
    square = jax.ShapeDtypeStruct((width, width), full)
    lengths = [width // 2] * 4 + [width] * 6 + [4 * width, HEADS * KERNEL // 2]
    return pl.pallas_call(
        finish_kernel,
        out_shape=[
            jax.ShapeDtypeStruct(grad_input.shape, full),
            jax.ShapeDtypeStruct(output.shape, low),
            square, square, square, square, square,
            jax.ShapeDtypeStruct((width, 2 * width), full),
            jax.ShapeDtypeStruct(inner_shape, full),
            jax.ShapeDtypeStruct(outer_shape, full),
            jax.ShapeDtypeStruct((KERNEL, width), full),
            jax.ShapeDtypeStruct((HEADS * KERNEL, width // 2), full),
        ] + [jax.ShapeDtypeStruct((n,), full) for n in lengths],
        in_specs=[pl.BlockSpec(memory_space=pltpu.SMEM)] + [anywhere] * 5,
        out_specs=[anywhere] * 10 + [vmem] * 14,
        scratch_shapes=[
            pltpu.VMEM(fin_ff.shape, low),
            pltpu.VMEM((PACK_A, width), low),
            pltpu.VMEM((PACK_B, width), low),
            pltpu.VMEM(grad_input.shape, full),
            pltpu.VMEM(output.shape, low),
            pltpu.VMEM((SMALL_AT, width), full),
            pltpu.VMEM((PACK_B, width), full),
            pltpu.VMEM((width, 2 * width), full),
            pltpu.VMEM(inner_shape, full),
            pltpu.VMEM(outer_shape, full),
            pltpu.SemaphoreType.DMA((5,)),
            pltpu.SemaphoreType.DMA((10,)),
        ],
        compiler_params=pltpu.CompilerParams(vmem_limit_bytes=60 * 2**20),
        name="finish",
    )(side, fin_ff, fin_a, fin_b, grad_input, output)


def on_device(
    hidden_in,
    segment_ids,
    out_grad,
    query_w,
    query_b,
    key_w,
    value_w,
    value_b,
    depth_kernel,
    point_w,
    point_b,
    kernel_w,
    kernel_b,
    conv_w,
    conv_b,
    output_w,
    output_b,
    norm1_gain,
    norm1_bias,
    inner_w,
    inner_b,
    outer_w,
    outer_b,
    norm2_gain,
    norm2_bias,
):
    micro_count, seq_local, block_len, model_width = hidden_in.shape
    seq_count = micro_count * seq_local
    att_width = HEADS * HEAD_DIM
    half_taps = KERNEL // 2
    position = lax.axis_index("ctx")
    seg_rows = segment_ids.reshape(seq_count, segment_ids.shape[2])
    pad_rows = (TEAM - 1) * block_len
    seg_pad = jnp.pad(seg_rows, ((0, 0), (pad_rows, pad_rows)), constant_values=-1)
    own_seg = lax.dynamic_slice_in_dim(seg_pad, position * block_len + pad_rows, block_len, 1)
    rank = lax.rem(position, TEAM)
    first_key = (position - rank) * block_len
    team_seg = lax.dynamic_slice(
        seg_pad, (lax.div(rank, 2), first_key), (1, (3 * TEAM - 2) * block_len)
    )
    key_place = first_key - pad_rows + lax.broadcasted_iota(jnp.int32, team_seg.shape, 1)
    team_seg = jnp.where(key_place >= seg_rows.shape[1], 2**24, team_seg)
    query_seg = team_seg[:, pad_rows : pad_rows + TEAM * block_len]
    lows = query_seg[0, ::TILE]
    highs = query_seg[0, TILE - 1 :: TILE]
    before = jnp.sum(team_seg < lows[:, None], axis=1, dtype=jnp.int32)
    through = jnp.sum(team_seg <= highs[:, None], axis=1, dtype=jnp.int32)
    bounds = jnp.stack([before // TILE, (through + TILE - 1) // TILE])
    seg_keys = team_seg.astype(jnp.float32)
    seg_queries = query_seg.astype(jnp.float32)
    rim_seg = lax.dynamic_slice_in_dim(
        seg_pad, position * block_len + pad_rows - RIM, block_len + 2 * RIM, 1
    )
    tap_mask = jnp.stack(
        [
            rim_seg[:, RIM - half_taps + j : RIM - half_taps + j + block_len] == own_seg
            for j in range(KERNEL)
        ],
        axis=1,
    ).astype(jnp.float32)
    seg_rim = jnp.pad(
        rim_seg.astype(jnp.float32), ((0, 0), (0, -rim_seg.shape[1] % LANES)), constant_values=-1
    )
    side = lax.axis_index("wsh")
    tap_rows = jnp.pad(tap_mask, ((0, 0), (0, 16 - KERNEL), (0, 0)))
    hidden = hidden_in.reshape(seq_count, block_len, model_width)
    (key_mat, value_mat, small_full, query_mat, point_mat, conv_mat, output_mat, inner_mat,
     window, query_team, queries, xrim, depth_low, span_keys, kern, ext, convolved,
     outer_half) = front(
        hidden, seg_rim, tap_rows, depth_kernel, kernel_w.T, kernel_b,
        [output_b, norm1_gain, norm1_bias, outer_b, norm2_gain, norm2_bias, inner_b],
        [query_b, value_b, point_b, conv_b],
        [key_w, value_w, query_w, point_w, conv_w, output_w, inner_w], outer_w,
    )
    outer_came = lax.ppermute(outer_half, "wsh", [(0, 1), (1, 0)])
    query_team = query_team.reshape(TEAM * block_len, 2 * LANES)
    attended_team, attended_t, log_sums = attend(
        bounds, query_team, window, seg_keys, seg_queries
    )
    (output, grad_sum1, grad_conv, grad_team, keep, xsend, vec_grads, bias_grads) = middle(
        attended_team.reshape(TEAM, block_len, -1), convolved, hidden, small_full,
        out_grad.reshape(seq_count, block_len, model_width),
        output_mat, inner_mat, outer_w, outer_came,
    )
    came = lax.ppermute(xsend, "ctx", [(i, i ^ 2) for i in range(lax.axis_size("ctx"))])
    grad_query_team, grad_window = attend_back(
        bounds, query_team, window, seg_keys, seg_queries,
        grad_team.reshape(TEAM * block_len, 2 * LANES), attended_t, log_sums,
    )
    grad_input, fin_ff, fin_a, fin_b = back(
        dict(seg=seg_rim, mask=tap_rows, small=small_full, vec=vec_grads, bias=bias_grads),
        grad_window, grad_query_team.reshape(TEAM, block_len, -1),
        dict(keep=keep, came=came, dconv=grad_conv, ext=ext, kern=kern, point=point_mat,
             queries=queries, spans=span_keys, depth=depth_low, xrim=xrim, x=hidden,
             convw=conv_mat, ds=grad_sum1, key=key_mat, value=value_mat, query=query_mat),
    )
    (grad_input, output, grad_query, grad_key, grad_value, grad_point, grad_conv, grad_output,
     grad_inner, grad_outer, grad_depth, grad_kernel, g_query_b, g_value_b, g_point_b, g_conv_b,
     g_output_b, gain1, shift1, g_outer_b, gain2, shift2, g_inner_b, g_kernel_b) = finish(
        side.astype(jnp.int32).reshape(1), fin_ff, fin_a, fin_b, grad_input, output,
        inner_w.shape, outer_w.shape,
    )
    return (
        output.reshape(hidden_in.shape), grad_input.reshape(hidden_in.shape),
        grad_query, g_query_b, grad_key, grad_value, g_value_b, grad_depth, grad_point,
        g_point_b, grad_kernel.T, g_kernel_b, grad_conv, g_conv_b, grad_output, g_output_b,
        gain1, shift1, grad_inner, g_inner_b, grad_outer, g_outer_b, gain2, shift2,
    )


def solution(mesh):
    in_specs = (
        P(None, "wsh", "ctx", None),
        P(None, "wsh", None),
        P(None, "wsh", "ctx", None),
        P("wsh", None),
        P("wsh"),
        P("wsh", None),
        P("wsh", None),
        P("wsh"),
        P(None, "wsh"),
        P("wsh", None),
        P("wsh"),
        P("wsh", None),
        P("wsh"),
        P("wsh", None),
        P("wsh"),
        P("wsh", None),
        P("wsh"),
        P("wsh"),
        P("wsh"),
        P(None, "wsh", None),
        P("wsh"),
        P(None, "wsh", None),
        P("wsh"),
        P("wsh"),
        P("wsh"),
    )
    out_specs = (
        P(None, "wsh", "ctx", None),
        P(None, "wsh", "ctx", None),
        P("wsh", None),
        P("wsh"),
        P("wsh", None),
        P("wsh", None),
        P("wsh"),
        P(None, "wsh"),
        P("wsh", None),
        P("wsh"),
        P("wsh", None),
        P("wsh"),
        P("wsh", None),
        P("wsh"),
        P("wsh", None),
        P("wsh"),
        P("wsh"),
        P("wsh"),
        P(None, "wsh", None),
        P("wsh"),
        P(None, "wsh", None),
        P("wsh"),
        P("wsh"),
        P("wsh"),
    )
    return jax.shard_map(
        on_device, mesh=mesh, in_specs=in_specs, out_specs=out_specs, check_vma=False
    )
```

profile of v0, /device:TPU:0, one launch (start us, length us, event | category | flops | bytes accessed | tf_op | source)
XLA Modules:
  0.0 281.2 jit_solution(10826742922883997338)
XLA Ops:
  0.7 0.9 copy.163
  1.6 0.1 dynamic-slice_convert_fusion
  1.7 0.1 compare_bitcast_fusion.1
  1.8 0.1 compare_bitcast_fusion
  2.1 0.1 stack.44
  2.2 0.6 pad_convert_fusion.refs_2_.refs_1_
  2.8 0.6 pad.15.refs_1_.refs_0_
  3.4 49.5 %front.1 = (bf16[768,384]{1,0:T(8,128)(2,1)}, bf16[768,384]{1,0:T(8,128)(2,1)}, bf16[256,384]{1,0:T(8,128)(2,1)}, bf16[768,384]{1,0:T(8,128)(2,1)}, bf16[768,384...) custom-call(bf16[2,512,768]{2,1,0:T(8,128)(2,1)} %bitcast.55, ...), custom_call_target="tpu_custom_call" | custom-call | tf_op jit(solution)/shard_map/front/pallas_call | solution.py:807
  52.9 0.6 collective-permute-start
  53.4 0.7 fusion
  54.2 0.6 slice_convert_fusion
  54.8 0.1 slice.47
  54.9 0.1 slice.46
  55.0 0.3 convert_reduce_fusion.1
  55.3 0.6 pad_add_fusion.bounds
  55.8 19.8 %attend.1 = (bf16[2048,256]{1,0:T(8,128)(2,1)}, f32[256,2048]{1,0:T(8,128)}, f32[8,2048]{1,0:T(8,128)}) custom-call(s32[2,8]{1,0:T(2,128)} %pad_add_fusion.bounds, bf16[2048,256]{1,0:T(8,128)(2,1)} %bitcast.58, bf16[5120,384]{1,0:T(8,128)(2,1)} %get-tuple-element.85.kv_ref, f32[1,5120]{1,0:T(1,128)} %get-tuple-element.408.segk_ref, ...), custom_call_target="tpu_custom_call" | custom-call | tf_op jit(solution)/shard_map/attend/pallas_call | solution.py:130
  75.6 0.0 collective-permute-done.uw_came
  75.6 0.0 copy-start
  75.6 0.8 copy-done
  76.4 46.4 %middle.1 = (bf16[2,512,768]{2,1,0:T(8,128)(2,1)}, f32[2,512,768]{2,1,0:T(8,128)}, bf16[2,512,384]{2,1,0:T(8,128)(2,1)}, bf16[4,512,256]{2,1,0:T(8,128)(2,1)}, f...) custom-call(bf16[4,512,256]{2,1,0:T(8,128)(2,1)} %bitcast.67, ...), custom_call_target="tpu_custom_call" | custom-call | tf_op jit(solution)/shard_map/middle/pallas_call | solution.py:1956
  122.8 0.3 collective-permute-start.1
  123.1 32.3 %attend_back.1 = (bf16[2048,256]{1,0:T(8,128)(2,1)}, bf16[5120,384]{1,0:T(8,128)(2,1)}) custom-call(s32[2,8]{1,0:T(2,128)} %pad_add_fusion.bounds, bf16[2048,256]{1,0:T(8,128)(2,1)} %bitcast.59, bf16[5120,384]{1,0:T(8,128)(2,1)} %get-tuple-element.85.kv_ref, f32[1,5120]{1,0:T(1,128)} %get-tuple-element.408.segk_ref, f32[1,2048]{1,0:T(1,128)} %get-tuple-element.419.segq_ref, ...), custom_call_target="tpu_custom_call" | custom-call | tf_op jit(solution)/shard_map/attend_back/pallas_call | solution.py:228
  155.3 2.4 collective-permute-done.1.refs_8_
  157.8 114.3 %back.1 = (f32[2,512,768]{2,1,0:T(8,128)}, bf16[3840,384]{1,0:T(8,128)(2,1)}, bf16[1280,384]{1,0:T(8,128)(2,1)}, bf16[768,384]{1,0:T(8,128)(2,1)}) custom-call(f32[2,640]{1,0:T(2,128)} %pad.15.refs_1_.refs_0_, f32[2,16,512]{2,1,0:T(8,128)} %pad_convert_fusion.refs_2_.refs_1_, bf16[256,384]{1,0:T(8,128)(2,1)} %get-tuple-element.83.small_ref.refs_2_, ...), custom_call_target="tpu_custom_call" | custom-call | tf_op jit(solution)/shard_map/back/pallas_call | solution.py:1655
  272.1 9.0 %finish.1 = (f32[2,512,768]{2,1,0:T(8,128)}, bf16[2,512,768]{2,1,0:T(8,128)(2,1)}, f32[384,384]{1,0:T(8,128)}, f32[384,384]{1,0:T(8,128)}, f32[384,384]{1,0:T(8,...) custom-call(s32[1]{0:T(128)} %bitcast.side_ref, ...), custom_call_target="tpu_custom_call" | custom-call | tf_op jit(solution)/shard_map/finish/pallas_call | solution.py:2095
  (10 shorter events, 0.1 us)
Async XLA Ops:
  52.9 22.7 %collective-permute-start = (bf16[2,384,384]{2,1,0:T(8,128)(2,1)}, bf16[2,384,384]{2,1,0:T(8,128)(2,1)S(1)}, u32[]{:S(2)}, u32[]{:S(2)}) collective-permute-start(bf16[2,384,384]{2,1,0:T(8,128)(2,1)} %get-tuple-element.90), channel_id=1, source_target_pairs={{0,1},{1,0},{2,3},{3,2},{4,5},{5,4},{6,7},{7,6},{8,9},{9,8},{10,11... | collective-permute-start | bytes 1769480 | tf_op jit(solution)/shard_map/ppermute | solution.py:2203
  75.6 0.8 copy-start
  122.8 35.0 %collective-permute-start.1 = (bf16[2,960,384]{2,1,0:T(8,128)(2,1)}, bf16[2,960,384]{2,1,0:T(8,128)(2,1)}, u32[]{:S(2)}, u32[]{:S(2)}) collective-permute-start(bf16[2,960,384]{2,1,0:T(8,128)(2,1)} %get-tuple-element.99), channel_id=1, source_target_pairs={{0,4},{2,6},{4,0},{6,2},{8,12},{10,14},{12,8},{14,10},{16,20},{18,... | collective-permute-start | bytes 4423688 | tf_op jit(solution)/shard_map/ppermute | solution.py:2213
where the time goes:
time: 282 us; the launch traced here: 281 us
  Pallas kernels  271 us (96%)
  other arithmetic  3.18 us (1%)
    pallas_call x1, Pallas kernels, back(): pl.pallas_call(kernel, out_shape=list(outs.values()) + fin_shapes, in_spe...  114 us
    pallas_call x1, Pallas kernels, front(): pl.pallas_call(functools.partial(front_kernel, count), out_shape=fulls +...  49.5 us
    pallas_call x1, Pallas kernels, middle(): pl.pallas_call(middle_kernel, out_shape=[jax.ShapeDtypeStruct((seqs, bloc...  46.4 us
    pallas_call x1, Pallas kernels, attend_back(): pl.pallas_call(attend_back_kernel, grid_spec=pltpu.PrefetchScalarGridSpec...  32.3 us
    pallas_call x1, Pallas kernels, attend(): pl.pallas_call(attend_kernel, grid_spec=pltpu.PrefetchScalarGridSpec(num_...  19.8 us
    pallas_call x1, Pallas kernels, finish(): pl.pallas_call(finish_kernel, out_shape=[jax.ShapeDtypeStruct(grad_input....  8.96 us
  transfers between devices with their start and end apart: 2, of which 1 were waited for; matrix products, arithmetic and copies ran while one was open for 1% of the time, Pallas kernels for 19%

commit v1 on v0

--- a/solution.py
+++ b/solution.py
@@ -56,17 +56,21 @@
 
 
 def over_tiles(first, last, step):
-    fours = lax.div(last - first, 4)
-
-    def four(p, carry):
-        step(first + 4 * p, 4)
+    sixes = lax.div(last - first, 6)
+
+    def six(p, carry):
+        step(first + 6 * p, 6)
         return carry
 
-    lax.fori_loop(0, fours, four, 0)
-    rest = last - first - 4 * fours
-    at = first + 4 * fours
-
-    @pl.when(rest >= 2)
+    lax.fori_loop(0, sixes, six, 0)
+    rest = last - first - 6 * sixes
+    at = first + 6 * sixes
+
+    @pl.when(rest >= 4)
+    def _():
+        step(at, 4)
+
+    @pl.when((rest == 2) | (rest == 3))
     def _():
         step(at, 2)
 

time: 282 us -> 278 us (0.986); the launches traced: 281 us -> 273 us
  Pallas kernels: 271 us -> 262 us
    pallas_call x1, Pallas kernels: 114 us -> 99.6 us  [back(): pl.pallas_call(kernel, out_shape=list(outs.values()) + fin_shapes, in_spe...]
    pallas_call x1, Pallas kernels: 46.4 us -> 52.4 us  [middle(): pl.pallas_call(middle_kernel, out_shape=[jax.ShapeDtypeStruct((seqs, bloc...]
where the time goes in v1:
time: 278 us; the launch traced here: 273 us
  Pallas kernels  262 us (94%)
  other arithmetic  3.18 us (1%)
    pallas_call x1, Pallas kernels, back(): pl.pallas_call(kernel, out_shape=list(outs.values()) + fin_shapes, in_spe...  99.6 us
    pallas_call x1, Pallas kernels, middle(): pl.pallas_call(middle_kernel, out_shape=[jax.ShapeDtypeStruct((seqs, bloc...  52.4 us
    pallas_call x1, Pallas kernels, front(): pl.pallas_call(functools.partial(front_kernel, count), out_shape=fulls +...  49.5 us
    pallas_call x1, Pallas kernels, attend_back(): pl.pallas_call(attend_back_kernel, grid_spec=pltpu.PrefetchScalarGridSpec...  32 us
    pallas_call x1, Pallas kernels, attend(): pl.pallas_call(attend_kernel, grid_spec=pltpu.PrefetchScalarGridSpec(num_...  19.7 us
    pallas_call x1, Pallas kernels, finish(): pl.pallas_call(finish_kernel, out_shape=[jax.ShapeDtypeStruct(grad_input....  8.96 us
  transfers between devices with their start and end apart: 2, of which 1 were waited for; matrix products, arithmetic and copies ran while one was open for 1% of the time, Pallas kernels for 19%

profile of v1, /device:TPU:0, one launch (start us, length us, event | category | flops | bytes accessed | tf_op | source)
XLA Modules:
  0.0 272.5 jit_solution(5276041135620717092)
XLA Ops:
  0.7 0.9 copy.163
  1.6 0.1 dynamic-slice_convert_fusion
  1.7 0.1 compare_bitcast_fusion.1
  1.8 0.1 compare_bitcast_fusion
  2.1 0.1 stack.44
  2.2 0.6 pad_convert_fusion.refs_2_.refs_1_
  2.8 0.6 pad.15.refs_1_.refs_0_
  3.4 49.5 %front.1 = (bf16[768,384]{1,0:T(8,128)(2,1)}, bf16[768,384]{1,0:T(8,128)(2,1)}, bf16[256,384]{1,0:T(8,128)(2,1)}, bf16[768,384]{1,0:T(8,128)(2,1)}, bf16[768,384...) custom-call(bf16[2,512,768]{2,1,0:T(8,128)(2,1)} %bitcast.55, ...), custom_call_target="tpu_custom_call" | custom-call | tf_op jit(solution)/shard_map/front/pallas_call | solution.py:811
  52.9 0.6 collective-permute-start
  53.4 0.7 fusion
  54.2 0.6 slice_convert_fusion
  54.8 0.1 slice.47
  54.9 0.1 slice.46
  55.0 0.3 convert_reduce_fusion.1
  55.3 0.6 pad_add_fusion.bounds
  55.8 19.7 %attend.1 = (bf16[2048,256]{1,0:T(8,128)(2,1)}, f32[256,2048]{1,0:T(8,128)}, f32[8,2048]{1,0:T(8,128)}) custom-call(s32[2,8]{1,0:T(2,128)} %pad_add_fusion.bounds, bf16[2048,256]{1,0:T(8,128)(2,1)} %bitcast.58, bf16[5120,384]{1,0:T(8,128)(2,1)} %get-tuple-element.85.kv_ref, f32[1,5120]{1,0:T(1,128)} %get-tuple-element.408.segk_ref, ...), custom_call_target="tpu_custom_call" | custom-call | tf_op jit(solution)/shard_map/attend/pallas_call | solution.py:134
  75.5 0.0 collective-permute-done.uw_came
  75.5 0.0 copy-start
  75.5 0.8 copy-done
  76.3 52.4 %middle.1 = (bf16[2,512,768]{2,1,0:T(8,128)(2,1)}, f32[2,512,768]{2,1,0:T(8,128)}, bf16[2,512,384]{2,1,0:T(8,128)(2,1)}, bf16[4,512,256]{2,1,0:T(8,128)(2,1)}, f...) custom-call(bf16[4,512,256]{2,1,0:T(8,128)(2,1)} %bitcast.67, ...), custom_call_target="tpu_custom_call" | custom-call | tf_op jit(solution)/shard_map/middle/pallas_call | solution.py:1960
  128.7 1.9 collective-permute-start.1
  130.6 32.0 %attend_back.1 = (bf16[2048,256]{1,0:T(8,128)(2,1)}, bf16[5120,384]{1,0:T(8,128)(2,1)}) custom-call(s32[2,8]{1,0:T(2,128)} %pad_add_fusion.bounds, bf16[2048,256]{1,0:T(8,128)(2,1)} %bitcast.59, bf16[5120,384]{1,0:T(8,128)(2,1)} %get-tuple-element.85.kv_ref, f32[1,5120]{1,0:T(1,128)} %get-tuple-element.408.segk_ref, f32[1,2048]{1,0:T(1,128)} %get-tuple-element.419.segq_ref, ...), custom_call_target="tpu_custom_call" | custom-call | tf_op jit(solution)/shard_map/attend_back/pallas_call | solution.py:232
  162.6 1.1 collective-permute-done.1.refs_8_
  163.8 99.6 %back.1 = (f32[2,512,768]{2,1,0:T(8,128)}, bf16[3840,384]{1,0:T(8,128)(2,1)}, bf16[1280,384]{1,0:T(8,128)(2,1)}, bf16[768,384]{1,0:T(8,128)(2,1)}) custom-call(f32[2,640]{1,0:T(2,128)} %pad.15.refs_1_.refs_0_, f32[2,16,512]{2,1,0:T(8,128)} %pad_convert_fusion.refs_2_.refs_1_, bf16[256,384]{1,0:T(8,128)(2,1)} %get-tuple-element.83.small_ref.refs_2_, ...), custom_call_target="tpu_custom_call" | custom-call | tf_op jit(solution)/shard_map/back/pallas_call | solution.py:1659
  263.3 9.0 %finish.1 = (f32[2,512,768]{2,1,0:T(8,128)}, bf16[2,512,768]{2,1,0:T(8,128)(2,1)}, f32[384,384]{1,0:T(8,128)}, f32[384,384]{1,0:T(8,128)}, f32[384,384]{1,0:T(8,...) custom-call(s32[1]{0:T(128)} %bitcast.side_ref, ...), custom_call_target="tpu_custom_call" | custom-call | tf_op jit(solution)/shard_map/finish/pallas_call | solution.py:2099
  (10 shorter events, 0.1 us)
Async XLA Ops:
  52.9 22.6 %collective-permute-start = (bf16[2,384,384]{2,1,0:T(8,128)(2,1)}, bf16[2,384,384]{2,1,0:T(8,128)(2,1)S(1)}, u32[]{:S(2)}, u32[]{:S(2)}) collective-permute-start(bf16[2,384,384]{2,1,0:T(8,128)(2,1)} %get-tuple-element.90), channel_id=1, source_target_pairs={{0,1},{1,0},{2,3},{3,2},{4,5},{5,4},{6,7},{7,6},{8,9},{9,8},{10,11... | collective-permute-start | bytes 1769480 | tf_op jit(solution)/shard_map/ppermute | solution.py:2207
  75.5 0.8 copy-start
  128.7 35.0 %collective-permute-start.1 = (bf16[2,960,384]{2,1,0:T(8,128)(2,1)}, bf16[2,960,384]{2,1,0:T(8,128)(2,1)}, u32[]{:S(2)}, u32[]{:S(2)}) collective-permute-start(bf16[2,960,384]{2,1,0:T(8,128)(2,1)} %get-tuple-element.99), channel_id=1, source_target_pairs={{0,4},{2,6},{4,0},{6,2},{8,12},{10,14},{12,8},{14,10},{16,20},{18,... | collective-permute-start | bytes 4423688 | tf_op jit(solution)/shard_map/ppermute | solution.py:2217
